TPU v7x, 32 devices: a whole 2x2x4 slice. The times are simulated.
32 devices in a mesh: dp: 4 (over y, x), expert: 8 (over z, core).
Axes of the slice: x: 2, y: 2, z: 4, core: 2. Of those that a mesh axis runs over, the one named last changes fastest.
Arguments:
- tokens: bfloat16 [10240, 1024], P(('dp', 'expert')), may hold values from -6 to 6
- attn_gain: bfloat16 [1024], P('dp'), may hold values from 0.5 to 1.5
- w_query: bfloat16 [1024, 1024], P('dp'), may hold values from -0.1875 to 0.1875
- w_keyval: bfloat16 [1024, 1024], P('dp'), may hold values from -0.1875 to 0.1875
- w_output: bfloat16 [1024, 1024], P('dp'), may hold values from -1.5 to 1.5
- moe_gain: bfloat16 [1024], P('dp'), may hold values from 0.5 to 1.5
- w_router: bfloat16 [1024, 32], P('dp'), may hold values from -0.09375 to 0.09375
- expert_in: bfloat16 [32, 1024, 1024], P('expert'), may hold values from -0.1875 to 0.1875
- expert_out: bfloat16 [32, 512, 1024], P('expert'), may hold values from -0.75 to 0.75
- cotangent: bfloat16 [10240, 1024], P(('dp', 'expert')), may hold values from -6 to 6
- routes: int32 [10240, 8], P(('dp', 'expert')), may hold values from 0 to 31, all different within a row; in each aligned block of 320 rows (0 to 319, 320 to 639, ...) at most 120 rows name the same one
- parents: int32 [32, 13], P(('dp', 'expert')), may hold values from 0 to 4, as said below
Outputs:
- block_out: bfloat16 [10240, 1024], P(('dp', 'expert'))
- input_grad: float32 [10240, 1024], P(('dp', 'expert'))
- grad_attn_gain: float32 [1024], P('dp')
- grad_w_query: float32 [1024, 1024], P('dp')
- grad_w_keyval: float32 [1024, 1024], P('dp')
- grad_w_output: float32 [1024, 1024], P('dp')
- grad_moe_gain: float32 [1024], P('dp')
- grad_w_router: float32 [1024, 32], P('dp')
- grad_expert_in: float32 [32, 1024, 1024], P('expert', 'dp')
- grad_expert_out: float32 [32, 512, 1024], P('expert', 'dp')
Inputs may be any that keep to these rules, and one draw needn't show every extreme that they name: `routes`: each row names 8 different experts. In each aligned block of 320 rows (the rows of one tree) no expert is named by more than 120 rows, and in some block one expert is named by exactly 120 rows. `parents`: in each tree, segments 0 to 4 have parent 0, and segments 5 to 12 name each of 1, 2, 3, 4 as parent exactly twice.
All inputs are finite; a program needn't handle non-finite values.
Results may differ from a plain program's by a relative error of at most 0.02.
Values may be sent and summed in bfloat16 or wider, within the bound.
A program may use at most 256 MiB of HBM per device.

v0:
```python
import functools

import jax
import jax.numpy as jnp
import numpy as np
from jax import lax
from jax.experimental import pallas as pl
from jax.experimental.pallas import tpu as pltpu
from jax.sharding import PartitionSpec as P

H = 16
KV = 8
HD = 64
EXPERTS = 32
TOPK = 8
CAP = 120


EPSILON = 1e-06


MESH = pl.DeviceIdType.MESH
MIB = 1024 * 1024
VMEM = pltpu.VMEM
ANY = pl.ANY


def remote(src, dst, send_sem, recv_sem, **where):
    return pltpu.make_async_remote_copy(
        src_ref=src, dst_ref=dst, send_sem=send_sem, recv_sem=recv_sem,
        device_id=where, device_id_type=MESH,
    )


def greet(partners):
    barrier = pltpu.get_barrier_semaphore()
    for condition, where in partners:
        def signal(where=where):
            pl.semaphore_signal(barrier, inc=1, device_id=where, device_id_type=MESH)
        if condition is None:
            signal()
        else:
            pl.when(condition)(signal)
    count = sum(1 if c is None else c.astype(jnp.int32) for c, _ in partners)
    pl.semaphore_wait(barrier, count)


def add_rows(out, *terms, step=16):
    rows = out.shape[0]

    def body(i, carry):
        at = pl.ds(pl.multiple_of(i * step, step), step)
        total = terms[0][at, :].astype(jnp.float32)
        for term in terms[1:]:
            total = total + term[at, :].astype(jnp.float32)
        out[at, :] = total.astype(out.dtype)
        return carry

    lax.fori_loop(0, rows // step, body, 0)


def bit_orders(n):
    bits = [1 << j for j in range(n.bit_length() - 1)]
    return [bits[p:] + bits[:p] for p in range(len(bits))] or [[]]


class Ring:
    def __init__(self, n_exp):
        self.mine = lax.axis_index("expert")
        self.core = lax.rem(self.mine, 2)
        self.z = lax.div(self.mine, 2)
        self.depth = n_exp // 2
        self.far = self.depth // 2
        self.pair = self.mine + 1 - 2 * self.core
        self.right, self.left = self.dev(1), self.dev(-1)

    def dev(self, d):
        return lax.rem(self.z + d + self.depth, self.depth) * 2 + self.core

    def partners(self):
        return [(None, {"expert": e}) for e in (self.pair, self.right, self.left)]


class RingGather:
    def __init__(self, ring, own, out, sems):
        self.ring, self.own, self.out = ring, own, out
        self.send, self.recv, self.pair_send, self.pair_recv = sems
        self.half = own.shape[0] // 2

    @staticmethod
    def scratch(n_exp):
        far, depth = n_exp // 4, n_exp // 2
        sem = pltpu.SemaphoreType.DMA
        return [sem((2, far + 1, 2)), sem((2, far + 1, 2)), sem((depth, 2)), sem((depth, 2))]

    def rows(self, h):
        return pl.ds(h * self.half, self.half)

    def goes(self, side, s, h):
        far = self.ring.far
        return s < far or (s == far and h == side)

    def block(self, d, h):
        return self.out.at[self.ring.dev(d), self.rows(h)]

    def hop(self, side, s, h):
        d = -s if side == 0 else s
        src = self.own.at[self.rows(h)] if s == 0 else self.block(d, h)
        to = self.ring.right if side == 0 else self.ring.left
        return remote(src, self.block(d, h), self.send.at[side, s, h], self.recv.at[side, s + 1, h], expert=to)

    def across(self, d, h):
        src = self.own.at[self.rows(h)] if d == 0 else self.block(d, h)
        slot = d % self.ring.depth
        return remote(src, self.block(d, h), self.pair_send.at[slot, h], self.pair_recv.at[slot, h], expert=self.ring.pair)

    ORDER = ((0, 0), (1, 1), (0, 1), (1, 0))

    def start(self):
        for side, h in self.ORDER:
            if self.goes(side, 1, h):
                self.hop(side, 0, h).start()
        self.across(0, 0).start()
        self.across(0, 1).start()

    def events(self):
        return [(side, s, h) for s in range(1, self.ring.far + 1) for side, h in self.ORDER if self.goes(side, s, h)]

    def handle(self, event):
        side, s, h = event
        d = -s if side == 0 else s
        here = self.block(d, h)
        remote(here, here, self.send.at[side, s, h], self.recv.at[side, s, h], expert=self.ring.mine).wait_recv()
        if self.goes(side, s + 1, h):
            self.hop(side, s, h).start()
        self.across(d, h).start()

    def wait_pair(self, d, h):
        slot = d % self.ring.depth
        here = self.out.at[self.ring.pair - self.ring.mine + self.ring.dev(d), self.rows(h)]
        remote(here, here, self.pair_send.at[slot, h], self.pair_recv.at[slot, h], expert=self.ring.mine).wait_recv()

    def finish_own(self):
        for side, h in self.ORDER:
            if self.goes(side, 1, h):
                self.hop(side, 0, h).wait_send()
        self.across(0, 0).wait_send()
        self.across(0, 1).wait_send()

    def finish_event(self, event):
        side, s, h = event
        if self.goes(side, s + 1, h):
            self.hop(side, s, h).wait_send()
        self.across(-s if side == 0 else s, h).wait_send()


class RingScatter:
    def __init__(self, ring, part, bufs, sems):
        self.ring, self.part = ring, part
        self.pair_buf, self.held, self.got = bufs
        self.pair_send, self.pair_recv, self.send, self.recv = sems
        self.half = self.held(0).shape[0] // 2

    @staticmethod
    def scratch(n_exp, block, dtype):
        far, depth = n_exp // 4, n_exp // 2
        sem = pltpu.SemaphoreType.DMA
        bufs = [pltpu.VMEM((depth,) + block, dtype), pltpu.VMEM((depth,) + block, dtype),
                pltpu.VMEM((2, far) + block, dtype)]
        return bufs, [sem((depth,)), sem((depth,)), sem((2, far + 1, 2)), sem((2, far + 1, 2))]

    def rows(self, h):
        return pl.ds(h * self.half, self.half)

    def order(self):
        far, depth = self.ring.far, self.ring.depth
        order = [far]
        for s in range(far - 1, 0, -1):
            order += [s, depth - s]
        return order + [0]

    def comes(self, side, d, h):
        far = self.ring.far
        return d + 1 < far or (d + 1 == far and h == side)

    def across(self, d):
        ring = self.ring
        return remote(self.part(d, 1), self.pair_buf(d),
                      self.pair_send.at[d], self.pair_recv.at[d], expert=ring.pair)

    def start_pair(self, d):
        self.across(d).start()

    def wait_pair(self, d):
        self.across(d).wait_recv()

    def wait_got(self, side, d, h):
        here = self.got(side, d).at[self.rows(h)]
        remote(here, here, self.send.at[side, d, h], self.recv.at[side, d, h], expert=self.ring.mine).wait_recv()

    def hop(self, side, d, h):
        slot = d if side == 0 else self.ring.depth - d
        rows = self.rows(h)
        return remote(self.held(slot).at[rows], self.got(side, d - 1).at[rows], self.send.at[side, d, h],
                      self.recv.at[side, d - 1, h], expert=self.ring.right if side == 0 else self.ring.left)

    def push(self, side, d, h):
        ring = self.ring
        slot = d if side == 0 else ring.depth - d
        rows = self.rows(h)
        terms = [self.part(slot, 0).at[rows], self.pair_buf(slot).at[rows]]
        if self.comes(side, d, h):
            self.wait_got(side, d, h)
            terms.append(self.got(side, d).at[rows])
        add_rows(self.held(slot).at[rows], *terms)
        self.hop(side, d, h).start()

    def first(self):
        far = self.ring.far
        self.wait_pair(far)
        self.push(0, far, 0)
        self.push(1, far, 1)

    def early(self):
        for d in range(self.ring.far - 1, 0, -1):
            self.wait_pair(d)
            self.push(0, d, 1)
            self.wait_pair(self.ring.depth - d)
            self.push(1, d, 0)

    def late(self):
        for d in range(self.ring.far - 1, 0, -1):
            self.push(0, d, 0)
            self.push(1, d, 1)

    def last(self, out, *more):
        self.wait_pair(0)
        for h in range(2):
            rows = self.rows(h)
            terms = [self.part(0, 0).at[rows], self.pair_buf(0).at[rows]] + [m.at[rows] for m in more]
            for side in range(2):
                if self.comes(side, 0, h):
                    self.wait_got(side, 0, h)
                    terms.append(self.got(side, 0).at[rows])
            add_rows(out.at[rows], *terms)

    def finish_sends(self):
        far = self.ring.far
        for side in range(2):
            for d in range(1, far + 1):
                for h in range(2):
                    if d < far or h == side:
                        self.hop(side, d, h).wait_send()
        for d in range(self.ring.depth):
            self.across(d).wait_send()


def views(bufs):
    pair_buf, held, got = bufs
    return (lambda d: pair_buf.at[d], lambda d: held.at[d], lambda side, d: got.at[side, d])


SLOTS = 128
F32, LOW = jnp.float32, jnp.bfloat16


def dot(a, b, over_a=1, over_b=0):
    return lax.dot_general(a, b, (((over_a,), (over_b,)), ((), ())), preferred_element_type=F32)


class ExpertSum:
    def __init__(self, me, first, half, land, send, recv):
        self.me, self.first, self.half, self.land, self.send, self.recv = me, first, half, land, send, recv

    def hop(self, step, h, which):
        bit = (1, 2)[h] if step == 0 else (2, 1)[h]
        r = bit if which == 0 else 3
        k = 2 * h + which if step == 0 else 4 + h
        src = self.first(r, h) if step == 0 else self.half(r, h)
        return remote(src, self.land(k), self.send(k), self.recv(k), dp=self.me ^ bit)

    def start(self, blocks=(1, 0)):
        for which in blocks:
            for h in range(2):
                self.hop(0, h, which).start()

    def turn(self, blocks=(1, 0)):
        for which in blocks:
            for h in range(2):
                self.hop(0, h, which).wait_recv()
                kept = 0 if which == 0 else (2, 1)[h]
                add_rows(self.half(kept, h), self.half(kept, h), self.land(2 * h + which))
                if which == 1:
                    self.hop(1, h, 0).start()

    def end(self, h, out):
        self.hop(1, h, 0).wait_recv()
        add_rows(out, self.half(0, h), self.land(4 + h))

    def finish(self):
        for step, h, which in ((0, 0, 0), (0, 0, 1), (0, 1, 0), (0, 1, 1), (1, 0, 0), (1, 1, 0)):
            self.hop(step, h, which).wait_send()


def experts_body(n_dp, n_exp, hid_ref, gy_hbm, routes_t, wr_t, w_in_hbm, w_out_hbm, middle,
                 block_out, hid_sum, gates_out, in_share, out_share, late,
                 x_all, w_in, w_out, sent, grows, gu, tmp, acts, stage, slots, gates, dots, wide,
                 pair_buf, held, got, *sems):
    w_sem, gy_sem, wide_sem, own_sem, ready, late_sem, gate_send, gate_recv, dp_ready, dp_send, dp_recv = sems[:11]
    gather_sems, out_sems, hid_sems = sems[11:15], sems[15:19], sems[19:23]
    me = lax.axis_index("dp")
    local, _, width = sent.shape
    tree, hidden_units = hid_ref.shape[0], w_out.shape[1]
    rows_e = local * SLOTS
    ring = Ring(n_exp)
    mine, core, depth = ring.mine, ring.core, ring.depth
    first = mine * local
    peers = [lax.rem(mine + k, n_exp) for k in range(1, n_exp)]
    greet([(None, {"expert": e}) for e in peers] + [(None, {"dp": me ^ bit}) for bit in (1, 2)])

    weights = [pltpu.make_async_copy(w_in_hbm, w_in, w_sem.at[0]), pltpu.make_async_copy(w_out_hbm, w_out, w_sem.at[1])]
    gather = RingGather(ring, hid_ref, x_all, gather_sems)
    gather.start()
    for copy in weights:
        copy.start()
    own = pltpu.make_async_copy(hid_ref, x_all.at[mine], own_sem)
    own.start()

    def gy_buf(j):
        return stage.at[lax.rem(j, 2), pl.ds(0, tree)]

    def gy_copy(j):
        return pltpu.make_async_copy(gy_hbm.at[j], gy_buf(j), gy_sem.at[lax.rem(j, 2)])

    gy_copy(0).start()

    below = (lax.broadcasted_iota(jnp.int32, (tree, tree), 0) < lax.broadcasted_iota(jnp.int32, (tree, tree), 1)).astype(LOW)
    sub16 = lax.broadcasted_iota(jnp.int32, (16, tree), 0)

    def find_slots(j, carry):
        names = routes_t[j]
        chosen = jnp.zeros((16, tree), F32)
        for k in range(names.shape[0]):
            chosen = jnp.maximum(chosen, jnp.where(names[k : k + 1, :] == first + sub16, 1.0, 0.0))
        chosen = jnp.where(sub16 < local, chosen, 0.0)
        rank = dot(chosen.astype(LOW), below)
        slots[j] = jnp.where(chosen > 0.5, rank, -1.0)[:8]
        return carry

    lax.fori_loop(0, n_exp, find_slots, 0)

    slot_ids = lax.broadcasted_iota(jnp.int32, (SLOTS, tree), 0).astype(F32)

    def places(j):
        return jnp.concatenate(
            [jnp.where(slot_ids == slots[j, i : i + 1, :], 1.0, 0.0).astype(LOW) for i in range(local)], axis=0)

    def places_t(j):
        lane = lax.broadcasted_iota(jnp.int32, (tree, 128), 1)
        pick = jnp.where(lax.broadcasted_iota(jnp.int32, (16, 128), 0) == lax.broadcasted_iota(jnp.int32, (16, 128), 1), 1.0, 0.0)
        slot = dot(jnp.concatenate([slots[j], jnp.zeros((8, tree), F32)], axis=0).astype(LOW), pick.astype(LOW), 0, 0)
        lanes = lane.astype(F32)
        return jnp.concatenate(
            [jnp.where(lanes == slot[:, i : i + 1], 1.0, 0.0).astype(LOW) for i in range(local)], axis=1)

    def find_gates(j):
        names = routes_t[j]
        experts = lax.broadcasted_iota(jnp.int32, (EXPERTS, tree), 0)
        chosen = jnp.zeros((EXPERTS, tree), F32)
        for k in range(names.shape[0]):
            chosen = jnp.maximum(chosen, jnp.where(names[k : k + 1, :] == experts, 1.0, 0.0))
        logits = jnp.where(chosen > 0.5, dot(wr_t[pl.ds(0, EXPERTS), :], x_all[j], 1, 1), -1e30)
        powers = jnp.exp(logits - jnp.max(logits, axis=0, keepdims=True))
        share = powers / jnp.sum(powers, axis=0, keepdims=True)
        sub = lax.broadcasted_iota(jnp.int32, (8, tree), 0)
        own_gates = jnp.zeros((8, tree), F32)
        for i in range(local):
            row = jnp.sum(jnp.where(experts == first + i, share, 0.0), axis=0, keepdims=True)
            own_gates = jnp.where(sub == i, row, own_gates)
        gates[j] = own_gates

    halves = width // 512

    def dispatch(j, src, dest):
        place = places(j)

        def body(n, carry):
            cols = pl.ds(pl.multiple_of(n * 512, 512), 512)
            picked = dot(place, src[:, cols]).astype(LOW)
            for i in range(local):
                dest[i, pl.ds(pl.multiple_of(j * SLOTS, SLOTS), SLOTS), cols] = picked[i * SLOTS : (i + 1) * SLOTS]
            return carry

        lax.fori_loop(0, halves, body, 0)

    def slot_gate(j, e):
        return jnp.sum(jnp.where(slot_ids == slots[j, pl.ds(e, 1), :], gates[j, pl.ds(e, 1), :], 0.0), axis=1, keepdims=True)

    def forward(chip):
        pair_rows = pl.ds(pl.multiple_of(chip * 2 * SLOTS, 2 * SLOTS), 2 * SLOTS)

        def one_tree(q, carry):
            j = 2 * chip + q
            find_gates(j)
            dispatch(j, x_all.at[j], sent)
            return carry

        lax.fori_loop(0, 2, one_tree, 0)

        def one_expert(e, carry):
            both = dot(sent[e, pair_rows, :], w_in[e])
            gu[e, pair_rows, :] = both.astype(LOW)
            a, b = both[:, :hidden_units], both[:, hidden_units:]
            act = (a / (1.0 + jnp.exp(-a)) * b).astype(LOW).astype(F32)
            gate = jnp.concatenate([slot_gate(2 * chip, e), slot_gate(2 * chip + 1, e)], axis=0)
            made = dot((act * gate).astype(LOW), w_out[e]).astype(LOW)
            for q in range(2):
                tmp[pl.ds(pl.multiple_of(q * rows_e + e * SLOTS, SLOTS), SLOTS), :] = made[q * SLOTS : (q + 1) * SLOTS]
            return carry

        lax.fori_loop(0, local, one_expert, 0)

    def combine_out(chip):
        def one_tree(q, carry):
            j = 2 * chip + q
            rows = pl.ds(pl.multiple_of(q * rows_e, rows_e), rows_e)
            x_all[j] = dot(places_t(j), tmp[rows, :]).astype(LOW)
            return carry

        lax.fori_loop(0, 2, one_tree, 0)

    def grad_rows(j, carry):
        pl.when(j + 1 < n_exp)(lambda: gy_copy(j + 1).start())
        gy_copy(j).wait()
        dispatch(j, gy_buf(j), grows)
        return carry

    events = gather.events()

    def out_part(d, other):
        return x_all.at[ring.dev(d) + other * (1 - 2 * core)]

    out = RingScatter(ring, out_part, views((pair_buf, held, got)), out_sems)

    def chip_at(d):
        return lax.rem(ring.z + d, depth)

    def group(g, carry):
        d = jnp.where(g == 0, 0, jnp.where(g == 1, depth - 1, jnp.where(g == 2, 1, 2)))
        chip = chip_at(d)

        @pl.when(g == 0)
        def _():
            own.wait()
            gather.wait_pair(0, 0)
            gather.wait_pair(0, 1)
            for copy in weights:
                copy.wait()

        @pl.when(g == 1)
        def _():
            for event in events[:4]:
                gather.handle(event)
            gather.wait_pair(-1, 0)
            gather.wait_pair(-1, 1)

        @pl.when(g == 2)
        def _():
            gather.wait_pair(1, 0)
            gather.wait_pair(1, 1)

        @pl.when(g == 3)
        def _():
            for event in events[4:]:
                gather.handle(event)
            gather.wait_pair(2, 0)
            gather.wait_pair(2, 1)

        forward(chip)

        @pl.when(g == 0)
        def _():
            gather.finish_own()
            lax.fori_loop(0, n_exp, grad_rows, 0)

        for at, d in ((1, -1), (2, 1), (3, 2)):
            @pl.when(g == at)
            def _():
                for event in events:
                    if event[1] == abs(d) and (abs(d) == 2 or (event[0] == 0) == (d < 0)):
                        gather.finish_event(event)

        combine_out(chip)
        pl.when(g == 0)(lambda: out.start_pair(0))
        pl.when(g == 1)(lambda: out.start_pair(depth - 1))
        pl.when(g == 2)(lambda: out.start_pair(1))
        pl.when(g == 3)(lambda: out.start_pair(2))
        return carry

    lax.fori_loop(0, depth, group, 0)
    out.first()
    out.early()
    middle_copy = pltpu.make_async_copy(middle, wide.at[pl.ds(0, tree)], wide_sem.at[0])
    middle_copy.start()

    in_rows, out_rows = width // n_dp, hidden_units // n_dp
    cut = (in_rows + out_rows) // 2

    def grad_half(e, r, h):
        at = 2 * r + h
        return gu.at[e, pl.ds(at * cut, cut)] if at < 5 else stage.at[e, pl.ds((at - 5) * cut, cut)]

    def grad_land(e, k):
        return w_in.at[e, pl.ds(k * cut, cut)] if k < 5 else w_out.at[e, pl.ds(0, cut)]

    def grad_sum(e):
        half = lambda r, h: grad_half(e, r, h)
        return ExpertSum(me, half, half, lambda k: grad_land(e, k), lambda k: dp_send.at[e, k], lambda k: dp_recv.at[e, k])

    def grads_start(e):
        pl.semaphore_wait(dp_ready.at[e], 2)
        grad_sum(e).start()

    def grads_turn(e):
        grad_sum(e).turn()

    def wide_copies(e):
        return (
            pltpu.make_async_copy(wide.at[pl.ds(0, in_rows)], in_share.at[e], wide_sem.at[0]),
            pltpu.make_async_copy(wide.at[pl.ds(in_rows, out_rows)], out_share.at[e], wide_sem.at[1]),
        )

    def grads_end(e):
        for h in range(2):
            grad_sum(e).end(h, wide.at[pl.ds(h * cut, cut)])
        for copy in wide_copies(e):
            copy.start()
        grad_sum(e).finish()
        for copy in wide_copies(e):
            copy.wait()

    block = 4 * SLOTS
    sub8 = lax.broadcasted_iota(jnp.int32, (8, tree), 0)

    def back_units(e):
        def one_block(m, inner):
            rows = pl.ds(pl.multiple_of(m * block, block), block)
            grad_act = dot(grows[e, rows, :], w_out[e], 1, 1)
            a = gu[e, rows, pl.ds(0, hidden_units)].astype(F32)
            b = gu[e, rows, pl.ds(hidden_units, hidden_units)].astype(F32)
            sg = 1.0 / (1.0 + jnp.exp(-a))
            sw = a * sg
            act = (sw * b).astype(LOW).astype(F32)
            gate = jnp.concatenate([slot_gate(4 * m + q, e) for q in range(4)], axis=0)
            told = jnp.sum(act * grad_act, axis=1, keepdims=True)
            acts[rows, :] = (act * gate).astype(LOW)
            grad_act = grad_act * gate
            tmp[rows, pl.ds(0, hidden_units)] = (grad_act * b * sg * (1.0 + a * (1.0 - sg))).astype(LOW)
            tmp[rows, pl.ds(hidden_units, hidden_units)] = (grad_act * sw).astype(LOW)
            for q in range(4):
                j = 4 * m + q
                row = jnp.sum(
                    jnp.where(slot_ids == slots[j, pl.ds(e, 1), :], told[q * SLOTS : (q + 1) * SLOTS], 0.0),
                    axis=0, keepdims=True)
                dots[j] = jnp.where(sub8 == e, row, dots[j])
            return inner

        lax.fori_loop(0, n_exp // 4, one_block, 0)

    def back_weights(e):
        for r in range(n_dp):
            d = me ^ r
            grad_in = dot(sent[e, :, pl.ds(pl.multiple_of(d * in_rows, in_rows), in_rows)], tmp[...], 0, 0).astype(LOW)
            grad_out = dot(acts[:, pl.ds(pl.multiple_of(d * out_rows, out_rows), out_rows)], grows[e], 0, 0).astype(LOW)
            grad_half(e, r, 0)[...] = grad_in[:cut]
            half = grad_half(e, r, 1)
            half[pl.ds(0, in_rows - cut), :] = grad_in[cut:]
            half[pl.ds(in_rows - cut, out_rows), :] = grad_out

    def back_rows(e, dest):
        def back_half(m, inner):
            rows = pl.ds(pl.multiple_of(m * 512, 512), 512)
            dest[rows, :] = dot(tmp[rows, :], w_in[e], 1, 1).astype(LOW)
            return inner

        lax.fori_loop(0, n_exp * SLOTS // 512, back_half, 0)

    end = local - 1

    def backward(e, carry):
        back_units(e)
        pl.when(e > 0)(lambda: grads_start(e - 1))
        back_weights(e)
        back_rows(e, sent.at[e])
        for bit in (1, 2):
            pl.semaphore_signal(dp_ready.at[e], inc=1, device_id={"dp": me ^ bit}, device_id_type=MESH)
        pl.when(e == 1)(out.late)
        pl.when(e >= 2)(lambda: grads_turn(e - 2))
        return carry

    dots[...] = jnp.zeros(dots.shape, F32)
    lax.fori_loop(0, end, backward, 0)
    back_units(end)
    grads_start(end - 1)
    back_rows(end, grows.at[end - 1])


    def hid_part(d, other):
        if d == 0:
            return x_all.at[mine + other * (1 - 2 * core)]
        k = 2 * (d - 1) + other
        return grows.at[k // 3, pl.ds((k % 3) * tree, tree)]

    hid = RingScatter(ring, hid_part, views((pair_buf, held, got)), hid_sems)

    def combine_hid(d):
        for other in range(2):
            j = ring.dev(d) + other * (1 - 2 * core)
            rows = pl.ds(pl.multiple_of(j * SLOTS, SLOTS), SLOTS)
            made = jnp.concatenate([sent[i, rows, :] for i in range(end)] + [grows[end - 1, rows, :]], axis=0)
            hid_part(d, other)[...] = dot(places_t(j), made).astype(LOW)

    for d in (2, 1, depth - 1):
        combine_hid(d)

    gate_copies = []
    for k, e in enumerate(peers):
        copy = remote(dots.at[e], gates_out.at[mine], gate_send.at[k], gate_recv.at[k], expert=e)
        copy.start()
        gate_copies.append(copy)
    gates_out[mine] = dots[mine]
    middle_copy.wait()
    out.last(block_out, wide.at[pl.ds(0, tree)])
    out.finish_sends()
    for partner in (ring.pair, ring.right, ring.left):
        pl.semaphore_signal(ready, inc=1, device_id={"expert": partner}, device_id_type=MESH)
    pl.semaphore_wait(ready, 3)
    for d in (2, 1, depth - 1):
        hid.start_pair(d)
    hid.first()
    combine_hid(0)
    hid.start_pair(0)
    hid.early()
    back_weights(end)

    def late_copy(r, h):
        at = pl.multiple_of((me ^ r) * 2 * cut + h * cut, 16)
        return pltpu.make_async_copy(grad_half(end, r, h), late.at[pl.ds(at, cut)], late_sem.at[2 * r + h])

    for r in range(n_dp):
        for h in range(2):
            late_copy(r, h).start()
    hid.late()
    grads_turn(end - 2)
    grads_end(0)
    grads_turn(end - 1)
    grads_end(1)
    hid.last(wide.at[pl.ds(0, tree)])
    hid_copy = pltpu.make_async_copy(wide.at[pl.ds(0, tree)], hid_sum, wide_sem.at[0])
    hid_copy.start()
    hid_copy.wait()
    for e in range(2, end):
        grads_end(e)
    for r in range(n_dp):
        for h in range(2):
            late_copy(r, h).wait()
    for k, copy in enumerate(gate_copies):
        copy.wait_send()
        source = lax.rem(mine + n_exp - 1 - k, n_exp)
        remote(dots.at[mine], gates_out.at[source], gate_send.at[k], gate_recv.at[k], expert=mine).wait_recv()
    hid.finish_sends()


def experts(n_dp, n_exp, hidden2, grad_y, routes_all, router_t, expert_in, expert_out, middle, collective_id):
    local, width, both = expert_in.shape
    units = expert_out.shape[1]
    tree = hidden2.shape[0]
    rows = n_exp * SLOTS
    sem = pltpu.SemaphoreType.DMA
    bufs, out_sems = RingScatter.scratch(n_exp, (tree, width), LOW)
    _, hid_sems = RingScatter.scratch(n_exp, (tree, width), LOW)
    shape = jax.ShapeDtypeStruct
    return pl.pallas_call(
        functools.partial(experts_body, n_dp, n_exp),
        out_shape=[
            shape((tree, width), LOW),
            shape((tree, width), F32),
            shape((n_exp, 8, tree), F32),
            shape((local - 1, width // n_dp, width), F32),
            shape((local - 1, units // n_dp, width), F32),
            shape((width + units, width), LOW),
        ],
        in_specs=[pl.BlockSpec(memory_space=s) for s in (VMEM, ANY, VMEM, VMEM, ANY, ANY, ANY)],
        out_specs=[pl.BlockSpec(memory_space=s) for s in (VMEM, ANY, VMEM, ANY, ANY, ANY)],
        scratch_shapes=[
            pltpu.VMEM((n_exp, tree, width), LOW),
            pltpu.VMEM((local, width, both), LOW),
            pltpu.VMEM((local, units, width), LOW),
            pltpu.VMEM((local, rows, width), LOW),
            pltpu.VMEM((local, rows, width), LOW),
            pltpu.VMEM((local, rows, both), LOW),
            pltpu.VMEM((max(rows, 2 * local * SLOTS), width), LOW),
            pltpu.VMEM((rows, units), LOW),
            pltpu.VMEM((local, 3 * (width + units) // (2 * n_dp), width), LOW),
            pltpu.VMEM((n_exp, 8, tree), F32),
            pltpu.VMEM((n_exp, 8, tree), F32),
            pltpu.VMEM((n_exp, 8, tree), F32),
            pltpu.VMEM(((width + units) // n_dp, width), F32),
            *bufs,
            sem((2,)), sem((2,)), sem((2,)), sem, pltpu.SemaphoreType.REGULAR, sem((2 * n_dp,)), sem((n_exp - 1,)), sem((n_exp - 1,)),
            pltpu.SemaphoreType.REGULAR((local,)), sem((local, 6)), sem((local, 6)),
            *RingGather.scratch(n_exp), *out_sems, *hid_sems,
        ],
        compiler_params=pltpu.CompilerParams(
            collective_id=collective_id, has_side_effects=True, vmem_limit_bytes=63 * MIB),
        name="experts",
    )(hidden2, grad_y, routes_all, router_t, expert_in, expert_out, middle)


def lanes_of(shape):
    return lax.broadcasted_iota(jnp.int32, shape, 1)


def turned(field):
    low_half = lax.rem(lanes_of(field.shape), HD) < HD // 2
    return jnp.where(low_half, -pltpu.roll(field, 128 - HD // 2, 1), pltpu.roll(field, HD // 2, 1))


def mask_bias(parents, tree):
    unit = tree // 20

    def segment(row):
        return jnp.where(row < 8 * unit, 0, jnp.where(row < 12 * unit, 1 + lax.div(row - 8 * unit, unit), 5 + lax.div(row - 12 * unit, unit)))

    count = parents.shape[1]
    names = parents[...].astype(F32)
    wide = (tree, count)
    seg = segment(lax.broadcasted_iota(jnp.int32, wide, 0)).astype(F32)
    lane = lanes_of(wide).astype(F32)
    own = seg[:, :1]
    parent = jnp.sum(jnp.where(lane == seg, names, 0.0), axis=1, keepdims=True)
    grand = jnp.sum(jnp.where(lane == parent, names, 0.0), axis=1, keepdims=True)
    square = (tree, tree)
    row, col = lax.broadcasted_iota(jnp.int32, square, 0), lanes_of(square)
    there = segment(col).astype(F32)
    hit = jnp.maximum(
        jnp.maximum(jnp.where(there == own, 1.0, 0.0), jnp.where(there == parent, 1.0, 0.0)), jnp.where(there == grand, 1.0, 0.0))
    hit = jnp.where(col <= row, hit, 0.0)
    return jnp.where(hit > 0.5, 0.0, -1e30)


def inverse_rms(field):
    return lax.rsqrt(jnp.mean(field * field, axis=-1, keepdims=True) + EPSILON)


class DpGather:
    def __init__(self, n_dp, mine, me, ins, outs, sems):
        self.n_dp, self.me, self.ins, self.outs = n_dp, me, ins, outs
        self.send, self.recv, self.pair_send, self.pair_recv, self.own_sem = sems
        self.core = lax.rem(mine, 2)
        self.pair = mine + 1 - 2 * self.core
        self.shard = ins[0].shape[0]
        half = self.shard // 2
        self.orders = bit_orders(n_dp)
        self.cuts = min(2, len(self.orders), half // 16)
        self.size = half // self.cuts

    @staticmethod
    def scratch(count, n_dp):
        sem = pltpu.SemaphoreType.DMA
        bits = max(1, n_dp.bit_length() - 1)
        return [sem((count, 2, n_dp, bits)), sem((count, 2, n_dp)), sem((count, 2, n_dp)), sem((count, 2, n_dp)), sem((count,))]

    def rows(self, start, side, p):
        return pl.ds(pl.multiple_of(start + side * (self.shard // 2) + p * self.size, 16), self.size)

    def hop(self, a, p, r, bit):
        there = self.outs[a].at[self.rows((self.me ^ r) * self.shard, self.core, p)]
        src = self.ins[a].at[self.rows(0, self.core, p)] if r == 0 else there
        return remote(src, there, self.send.at[a, p, r, bit.bit_length() - 1], self.recv.at[a, p, r ^ bit], dp=self.me ^ bit)

    def own(self, a):
        at = pl.ds(pl.multiple_of(self.me * self.shard, 16), self.shard)
        return pltpu.make_async_copy(self.ins[a], self.outs[a].at[at], self.own_sem.at[a])

    def across(self, a, p, r, side):
        here = self.outs[a].at[self.rows((self.me ^ r) * self.shard, side, p)]
        return remote(here, here, self.pair_send.at[a, p, r], self.pair_recv.at[a, p, r], expert=self.pair)

    def start(self, a):
        for p in range(self.cuts):
            for bit in self.orders[p]:
                self.hop(a, p, 0, bit).start()
        self.own(a).start()

    def stage(self, p, j):
        order = self.orders[p]
        blocks = [0]
        for bit in order[:j]:
            blocks = blocks + [r | bit for r in blocks]
        return [r | order[j] for r in blocks], order[j + 1 :]

    def turn(self, a, j):
        for p in range(self.cuts):
            blocks, onward = self.stage(p, j)
            for r in blocks:
                here = self.outs[a].at[self.rows((self.me ^ r) * self.shard, self.core, p)]
                remote(here, here, self.send.at[a, p, r, 0], self.recv.at[a, p, r], dp=self.me).wait_recv()
                for bit in onward:
                    self.hop(a, p, r, bit).start()
                self.across(a, p, r, self.core).start()

    def ready(self, a):
        self.own(a).wait()
        for p in range(self.cuts):
            for r in range(1, self.n_dp):
                self.across(a, p, r, 1 - self.core).wait_recv()

    def finish(self, a):
        for p in range(self.cuts):
            for bit in self.orders[p]:
                self.hop(a, p, 0, bit).wait_send()
            for j in range(len(self.orders[p])):
                blocks, onward = self.stage(p, j)
                for r in blocks:
                    for bit in onward:
                        self.hop(a, p, r, bit).wait_send()
                    self.across(a, p, r, self.core).wait_send()


def front_body(n_dp, n_exp, x_ref, gain_pair, router_in, w_query, w_keyval, w_output, routes_t, parents, cosine, sine, cot,
               hidden_hbm, queries_hbm, keys_hbm, values_hbm, attended, middle, hidden2, log_total,
               query_hbm, keyval_hbm, output_hbm, router_t, gains, routes_all, grad_y,
               hidden, queries, keys, values, query_full, keyval_full, output_full, small, small_all, bias, *sems):
    gather_sems, (small_send, small_recv, route_send, route_recv, out_sem), ring_sems = sems[:5], sems[5:10], sems[10:14]
    me, mine = lax.axis_index("dp"), lax.axis_index("expert")
    peers = [lax.rem(mine + k, n_exp) for k in range(1, n_exp)]
    greet([(None, {"expert": e}) for e in peers] + [(None, {"dp": me ^ k}) for k in range(1, n_dp)])
    tree, width = x_ref.shape
    shard = w_query.shape[0]

    small[...] = jnp.zeros(small.shape, LOW)
    small[pl.ds(0, EXPERTS), :] = router_in[...]
    sub = lax.broadcasted_iota(jnp.int32, (16, shard), 0)
    gain_rows = gain_pair[...].astype(F32)
    small[pl.ds(EXPERTS, 16), :] = jnp.where(sub == 0, gain_rows[:1], jnp.where(sub == 1, gain_rows[1:], 0.0)).astype(LOW)

    gather = DpGather(n_dp, mine, me, (w_query, w_keyval, w_output), (query_full, keyval_full, output_full), gather_sems)

    def small_copy(k):
        return remote(small, small_all.at[me], small_send.at[k], small_recv.at[k], dp=me ^ k)

    def route_copy(k, e):
        return remote(routes_t, routes_all.at[mine], route_send.at[k], route_recv.at[k], expert=e)

    saves = [
        pltpu.make_async_copy(src, dst, out_sem.at[k])
        for k, (src, dst) in enumerate((
            (query_full, query_hbm), (keyval_full, keyval_hbm), (output_full, output_hbm), (hidden, hidden_hbm),
            (queries, queries_hbm), (keys, keys_hbm), (values, values_hbm), (cot, grad_y.at[mine])))
    ]
    ring = RingGather(Ring(n_exp), cot, grad_y, ring_sems)
    events = ring.events()
    for k in range(1, n_dp):
        small_copy(k).start()
    ring.start()
    gather.start(0)
    gather.start(1)
    saves[7].start()
    for k, e in enumerate(peers):
        route_copy(k, e).start()
    small_all[me] = small[...]
    routes_all[mine] = routes_t[...]
    bias[...] = mask_bias(parents, tree)
    log_total[...] = jnp.zeros(log_total.shape, F32)
    x = x_ref[...].astype(F32)
    scaled = x * inverse_rms(x)
    for k in range(1, n_dp):
        remote(small, small_all.at[me ^ k], small_send.at[k], small_recv.at[k], dp=me).wait_recv()
    joined = jnp.concatenate([small_all[d] for d in range(n_dp)], axis=1)
    router_t[...] = jnp.zeros(router_t.shape, LOW)
    router_t[pl.ds(0, EXPERTS), :] = joined[:EXPERTS]
    gains[...] = joined[EXPERTS:]
    gain_rows = joined[EXPERTS:].astype(F32)
    hidden[...] = (scaled * gain_rows[:1]).astype(LOW)
    saves[3].start()
    stages = len(gather.orders[0])
    for j in range(stages - 1):
        gather.turn(0, j)
        gather.turn(1, j)
    gather.start(2)
    gather.turn(0, stages - 1)
    gather.turn(1, stages - 1)
    for event in events[:2]:
        ring.handle(event)
    gather.ready(0)
    saves[0].start()

    def rotate(field):
        return field * cosine[...] + turned(field) * sine[...]

    left = lanes_of((tree, 128)) < HD
    tile = 512

    def query_tile(n, carry):
        cols = pl.ds(pl.multiple_of(n * tile, tile), tile)
        pre = dot(hidden[...], query_full[:, cols])
        for i in range(tile // 128):
            at = pl.multiple_of(n * tile + i * 128, 128)
            queries[:, pl.ds(at, 128)] = rotate(pre[:, i * 128 : (i + 1) * 128]).astype(LOW)
        return carry

    lax.fori_loop(0, width // tile, query_tile, 0)
    saves[4].start()
    gather.ready(1)
    saves[1].start()

    def spread(field, out, i):
        other = pltpu.roll(field, HD, 1)
        out[2 * i] = jnp.where(left, field, other).astype(LOW)
        out[2 * i + 1] = jnp.where(left, other, field).astype(LOW)

    half = KV * HD
    pre = dot(hidden[...], keyval_full[:, pl.ds(0, half)])
    for i in range(half // 128):
        spread(rotate(pre[:, i * 128 : (i + 1) * 128]), keys, i)
    saves[5].start()
    pre = dot(hidden[...], keyval_full[:, pl.ds(half, half)])
    for i in range(half // 128):
        spread(pre[:, i * 128 : (i + 1) * 128], values, i)
    saves[6].start()
    for j in range(stages):
        gather.turn(2, j)

    def heads(c, carry):
        cols = pl.ds(pl.multiple_of(c * 128, 128), 128)
        pair = queries[:, cols]
        made = []
        for h in range(2):
            mine_lanes = left if h == 0 else jnp.logical_not(left)
            query = jnp.where(mine_lanes, pair, jnp.zeros_like(pair))
            scores = dot(query, keys[c], 1, 1) * HD**-0.5 + bias[...]
            top = jnp.max(scores, axis=1, keepdims=True)
            powers = jnp.exp(scores - top)
            total = jnp.sum(powers, axis=1, keepdims=True)
            made.append(dot((powers / total).astype(LOW), values[c]))
            log_total[...] = jnp.where(lanes_of((tree, 128)) == 2 * c + h, top + jnp.log(total), log_total[...])
        attended[:, cols] = jnp.where(left, made[0], made[1]).astype(LOW)
        return carry

    lax.fori_loop(0, KV, heads, 0)
    for event in events[2:4]:
        ring.handle(event)
    gather.ready(2)
    saves[2].start()

    def middle_tile(n, carry):
        cols = pl.ds(pl.multiple_of(n * tile, tile), tile)
        middle[:, cols] = x_ref[:, cols].astype(F32) + dot(attended[...], output_full[:, cols])
        return carry

    lax.fori_loop(0, width // tile, middle_tile, 0)
    field = middle[...]
    hidden2[...] = (field * inverse_rms(field) * gain_rows[1:2]).astype(LOW)
    for a in range(3):
        gather.finish(a)
    for k in range(1, n_dp):
        small_copy(k).wait_send()
    for k, e in enumerate(peers):
        route_copy(k, e).wait_send()
        source = lax.rem(mine + n_exp - 1 - k, n_exp)
        remote(routes_t, routes_all.at[source], route_send.at[k], route_recv.at[k], expert=mine).wait_recv()
    for event in events[4:]:
        ring.handle(event)
    ring.finish_own()
    for h in range(2):
        ring.wait_pair(0, h)
    for event in events:
        ring.finish_event(event)
        ring.wait_pair(-event[1] if event[0] == 0 else event[1], event[2])
    for copy in saves:
        copy.wait()


def front(n_dp, n_exp, tokens, gain_pair, router_in, w_query, w_keyval, w_output, routes_t, parents, tables, cot, collective_id):
    tree, width = tokens.shape
    shard = w_query.shape[0]
    shape, sem, vm = jax.ShapeDtypeStruct, pltpu.SemaphoreType.DMA, pltpu.VMEM
    low = shape((tree, width), LOW)
    spread = shape((KV, tree, 128), LOW)
    full = shape((n_dp * shard, width), LOW)
    small = (EXPERTS + 16, shard)
    return pl.pallas_call(
        functools.partial(front_body, n_dp, n_exp),
        out_shape=[
            low, low, spread, spread, low, shape((tree, width), F32), low, shape((tree, 128), F32),
            full, full, full, shape((128, width), LOW), shape((16, width), LOW),
            shape((n_exp,) + routes_t.shape, jnp.int32), shape((n_exp, tree, width), LOW),
        ],
        in_specs=[pl.BlockSpec(memory_space=VMEM)] * 11,
        out_specs=[pl.BlockSpec(memory_space=s) for s in [ANY] * 4 + [VMEM] * 4 + [ANY] * 3 + [VMEM] * 3 + [ANY]],
        scratch_shapes=[
            vm((tree, width), LOW), vm((tree, width), LOW), vm(spread.shape, LOW), vm(spread.shape, LOW),
            vm(full.shape, LOW), vm(full.shape, LOW), vm(full.shape, LOW),
            vm(small, LOW), vm((n_dp,) + small, LOW), vm((tree, tree), F32),
            *DpGather.scratch(3, n_dp), sem((n_dp,)), sem((n_dp,)), sem((n_exp - 1,)), sem((n_exp - 1,)), sem((8,)),
            *RingGather.scratch(n_exp),
        ],
        compiler_params=pltpu.CompilerParams(
            collective_id=collective_id, has_side_effects=True, vmem_limit_bytes=56 * MIB),
        name="front",
    )(tokens, gain_pair, router_in, w_query, w_keyval, w_output, routes_t, parents, *tables, cot)


class GradSum:
    def __init__(self, n_dp, n_exp, chunks, own, bufs, sems):
        self.n_dp, self.chunks, self.own = n_dp, chunks, own
        (self.pair_in, self.dp_in, self.prefix, self.suffix, self.go_r, self.go_l, self.final, self.other) = bufs
        (self.pair_send, self.pair_recv, self.dp_send, self.dp_recv,
         self.send_r, self.send_l, self.recv_r, self.recv_l, self.last_send, self.last_recv) = sems
        self.me, self.mine = lax.axis_index("dp"), lax.axis_index("expert")
        self.core = lax.rem(self.mine, 2)
        self.z = lax.div(self.mine, 2)
        self.depth = n_exp // 2
        self.pair = self.mine + 1 - 2 * self.core
        self.has_left, self.has_right = self.z > 0, self.z < self.depth - 1
        self.orders = bit_orders(n_dp)

    @staticmethod
    def scratch(n_dp, chunks, half, columns):
        sem = pltpu.SemaphoreType.DMA
        stages = max(1, n_dp.bit_length() - 1)
        one = pltpu.VMEM((chunks, half, columns), LOW)
        many = pltpu.VMEM((chunks, n_dp, half, columns), LOW)
        bufs = [many, many, one, one, one, one, one, one]
        sems = [sem((chunks, n_dp)), sem((chunks, n_dp)), sem((chunks, n_dp)), sem((chunks, n_dp))]
        return bufs, sems + [sem((chunks,))] * 6

    def partners(self):
        return [(None, {"dp": self.me ^ bit}) for bit in self.orders[0]] + [
            (self.has_left, {"expert": self.mine - 2}), (self.has_right, {"expert": self.mine + 2})]

    def total(self, i, r):
        return self.own.at[i, self.me ^ r, self.core]

    def across(self, i, d):
        return remote(self.own.at[i, d, 1 - self.core], self.pair_in.at[i, d], self.pair_send.at[i, d],
                      self.pair_recv.at[i, d], expert=self.pair)

    def moved(self, i, j):
        order = self.orders[i % len(self.orders)]
        blocks = [0]
        for bit in order[j + 1 :]:
            blocks = blocks + [r | bit for r in blocks]
        return order[j], [r | order[j] for r in blocks]

    def dp_copy(self, i, r, bit):
        return remote(self.total(i, r), self.dp_in.at[i, r], self.dp_send.at[i, r], self.dp_recv.at[i, r], dp=self.me ^ bit)

    def start(self, i):
        for d in range(self.n_dp):
            self.across(i, d).start()

    def paired(self, i):
        for r in range(self.n_dp - 1, -1, -1):
            d = self.me ^ r
            self.across(i, d).wait_recv()
            add_rows(self.total(i, r), self.total(i, r), self.pair_in.at[i, d])
        self.leave(i, 0)

    def leave(self, i, j):
        if j < len(self.orders[0]):
            bit, blocks = self.moved(i, j)
            for r in blocks:
                self.dp_copy(i, r, bit).start()

    def met(self, i, j):
        bit, blocks = self.moved(i, j)
        for r in blocks:
            self.dp_copy(i, r, bit).wait_recv()
            add_rows(self.total(i, r ^ bit), self.total(i, r ^ bit), self.dp_in.at[i, r])
        self.leave(i, j + 1)

    def right(self, i):
        return remote(self.go_r.at[i], self.prefix.at[i], self.send_r.at[i], self.recv_r.at[i], expert=self.mine + 2)

    def left(self, i):
        return remote(self.go_l.at[i], self.suffix.at[i], self.send_l.at[i], self.recv_l.at[i], expert=self.mine - 2)

    def line(self, t):
        i = t - 2 * self.z
        has_left, has_right = self.has_left, self.has_right

        @pl.when(jnp.logical_and(i >= 0, i < self.chunks))
        def _():
            @pl.when(has_left)
            def _():
                remote(self.go_r.at[i], self.prefix.at[i], self.send_r.at[i], self.recv_r.at[i], expert=self.mine).wait_recv()

            @pl.when(jnp.logical_and(has_left, has_right))
            def _():
                add_rows(self.go_r.at[i], self.total(i, 0), self.prefix.at[i])

            @pl.when(jnp.logical_not(has_left))
            def _():
                add_rows(self.go_r.at[i], self.total(i, 0))

            pl.when(has_right)(lambda: self.right(i).start())

        k = t - 2 * (self.depth - 1 - self.z)

        @pl.when(jnp.logical_and(k >= 0, k < self.chunks))
        def _():
            @pl.when(has_right)
            def _():
                remote(self.go_l.at[k], self.suffix.at[k], self.send_l.at[k], self.recv_l.at[k], expert=self.mine).wait_recv()

            @pl.when(jnp.logical_and(has_left, has_right))
            def _():
                add_rows(self.go_l.at[k], self.total(k, 0), self.suffix.at[k])

            @pl.when(jnp.logical_not(has_right))
            def _():
                add_rows(self.go_l.at[k], self.total(k, 0))

            pl.when(has_left)(lambda: self.left(k).start())

    def last(self, i):
        return remote(self.final.at[i], self.other.at[i], self.last_send.at[i], self.last_recv.at[i], expert=self.pair)

    def close(self, i):
        has_left, has_right = self.has_left, self.has_right

        @pl.when(jnp.logical_and(has_left, has_right))
        def _():
            add_rows(self.final.at[i], self.total(i, 0), self.prefix.at[i], self.suffix.at[i])

        @pl.when(jnp.logical_not(has_left))
        def _():
            add_rows(self.final.at[i], self.total(i, 0), self.suffix.at[i])

        @pl.when(jnp.logical_not(has_right))
        def _():
            add_rows(self.final.at[i], self.total(i, 0), self.prefix.at[i])

        self.last(i).start()

    def finish(self, i):
        self.last(i).wait_send()
        pl.when(self.has_right)(lambda: self.right(i).wait_send())
        pl.when(self.has_left)(lambda: self.left(i).wait_send())
        for d in range(self.n_dp):
            self.across(i, d).wait_send()
        for j in range(len(self.orders[0])):
            bit, blocks = self.moved(i, j)
            for r in blocks:
                self.dp_copy(i, r, bit).wait_send()


def two_parts(field):
    high = field.astype(LOW)
    return high, (field - high.astype(F32)).astype(LOW)


def norm_back(field, gain, grad):
    r = inverse_rms(field)
    scaled = grad * gain
    back = r * scaled - field * (r * r * r) * jnp.mean(field * scaled, axis=-1, keepdims=True)
    return back, jnp.sum(field * r * grad, axis=0, keepdims=True)


def back_body(n_dp, n_exp, local, with_late, x_ref, cot, hid_sum, gates_in, routes_t, parents, cosine, sine,
              hidden, queries, keys, values, attended, middle, hidden2, log_total,
              query_hbm, keyval_hbm, output_hbm, router_t, gains, *refs):
    if with_late:
        late_hbm, refs = refs[0], refs[1:]
    outs, refs = refs[: 5 + 2 * with_late], refs[5 + 2 * with_late :]
    input_grad, grad_q, grad_kv, grad_o, grad_s = outs[:5]
    (bias, branch, grad_att, grad_q_pre, grad_kv_pre, rhs, own, own_s, grad_hid, query_full, keyval_full, output_full,
     load_sem, *rest) = refs
    big = GradSum(n_dp, n_exp, own.shape[0], own, rest[:8], rest[8:18])
    little = GradSum(n_dp, n_exp, 1, own_s, rest[18:26], rest[26:36])
    tree, width = x_ref.shape
    ring = Ring(n_exp)
    greet(big.partners() + [(None, {"expert": ring.pair})])
    loads = [
        pltpu.make_async_copy(src, dst, load_sem.at[k])
        for k, (src, dst) in enumerate(((output_hbm, output_full), (query_hbm, query_full), (keyval_hbm, keyval_full)))
    ]
    if with_late:
        late_sem, late_send, late_recv, wide_sem, late_buf = rest[36:41]
        cut = late_hbm.shape[0] // (2 * n_dp)
        kept = {(0, 0): 0, (0, 1): 1, (2, 0): 2, (1, 1): 3}

        def late_rows(r, h):
            return late_hbm.at[pl.ds(pl.multiple_of((big.me ^ r) * 2 * cut + h * cut, 16), cut)]

        def late_half(r, h):
            return late_buf.at[pl.ds(kept[r, h] * cut, cut)]

        def late_land(k):
            return late_buf.at[pl.ds((4 + k) * cut, cut)]

        late = ExpertSum(big.me, late_rows, late_half, late_land, lambda k: late_send.at[k], lambda k: late_recv.at[k])
        late.start()
        late_loads = [pltpu.make_async_copy(late_rows(r, h), late_half(r, h), late_sem.at[k]) for (r, h), k in kept.items()]
        for copy in late_loads:
            copy.start()
        in_rows = outs[5].shape[0]

        def late_end():
            for h in range(2):
                late.end(h, grad_hid.at[pl.ds(0, cut)])
                if h == 0:
                    copies = [pltpu.make_async_copy(grad_hid.at[pl.ds(0, cut)], outs[5].at[pl.ds(0, cut)], wide_sem.at[0])]
                else:
                    copies = [
                        pltpu.make_async_copy(grad_hid.at[pl.ds(0, in_rows - cut)], outs[5].at[pl.ds(cut, in_rows - cut)], wide_sem.at[0]),
                        pltpu.make_async_copy(grad_hid.at[pl.ds(in_rows - cut, 2 * cut - in_rows)], outs[6], wide_sem.at[1])]
                for copy in copies:
                    copy.start()
                for copy in copies:
                    copy.wait()
            late.finish()

    for copy in loads:
        copy.start()
    shard = width // n_dp
    side = shard // 2
    tile = 512
    lane = lanes_of((tree, 128))
    left = lane < HD

    def gain_row(i):
        return gains[...].astype(F32)[i : i + 1]

    bias[...] = mask_bias(parents, tree)

    names = routes_t[...].astype(F32)
    pick = jnp.where(lax.broadcasted_iota(jnp.int32, (16, 128), 0) == lanes_of((16, 128)), 1.0, 0.0).astype(LOW)
    names = dot(jnp.concatenate([names, jnp.zeros_like(names)], axis=0).astype(LOW), pick, 0, 0)
    chosen = jnp.zeros((tree, 128), F32)
    for k in range(routes_t.shape[0]):
        chosen = jnp.maximum(chosen, jnp.where(names[:, k : k + 1] == lane.astype(F32), 1.0, 0.0))
    logits = jnp.where(chosen > 0.5, dot(hidden2[...], router_t[...], 1, 1), -1e30)
    powers = jnp.exp(logits - jnp.max(logits, axis=1, keepdims=True))
    gate = powers / jnp.sum(powers, axis=1, keepdims=True)
    count = gates_in.shape[0]
    where_row = lax.broadcasted_iota(jnp.int32, (count, 128), 0)
    where_lane = lanes_of((count, 128))
    group_row = lax.rem(where_row, 8)
    target = lax.div(where_row, 8) * local + group_row
    pick = jnp.where(group_row < local, jnp.where(target == where_lane, 1.0, 0.0), 0.0).astype(LOW)
    high, low = two_parts(gates_in[...])
    gate_back = dot(high, pick, 0, 0) + dot(low, pick, 0, 0)
    grad_logits = (gate * (gate_back - jnp.sum(gate * gate_back, axis=1, keepdims=True))).astype(LOW)
    grad_router = dot(grad_logits, hidden2[...], 0, 0)[:EXPERTS]
    grad_hidden2 = hid_sum[...] + dot(grad_logits, router_t[...])
    back, gain2_sum = norm_back(middle[...], gain_row(1), grad_hidden2)
    grad_middle = cot[...].astype(F32) + back
    input_grad[...] = grad_middle
    branch[...] = grad_middle.astype(LOW)

    def chunk_grads(i, lhs, rhs_ref):
        def part(n, carry):
            made = dot(lhs[:, pl.ds(pl.multiple_of(n * tile, tile), tile)], rhs_ref[...], 0, 0).astype(LOW)
            for k in range(tile // side):
                own[i, n * (tile // shard) + k // 2, k % 2] = made[k * side : (k + 1) * side]
            return carry

        if tile % shard == 0:
            lax.fori_loop(0, width // tile, part, 0)

    for i in range(2):
        rhs[...] = branch[:, pl.ds(i * tile, tile)]
        chunk_grads(i, attended, rhs)
        big.start(i)

    loads[0].wait()

    def att_tile(n, carry):
        rows = pl.ds(pl.multiple_of(n * tile, tile), tile)
        grad_att[:, rows] = dot(branch[...], output_full[rows, :], 1, 1).astype(LOW)
        return carry

    lax.fori_loop(0, width // tile, att_tile, 0)

    def unrotate(field):
        return field * cosine[...] - turned(field * sine[...])

    scale = HD**-0.5

    def group(c):
        cols = pl.ds(pl.multiple_of(c * 128, 128), 128)
        pair, grad_pair = queries[:, cols], grad_att[:, cols]
        zero = jnp.zeros_like(pair)
        key, value = keys[c], values[c]
        grad_query, grad_key, grad_value = [], 0.0, 0.0
        for h in range(2):
            here = left if h == 0 else jnp.logical_not(left)
            query, grad_out = jnp.where(here, pair, zero), jnp.where(here, grad_pair, zero)
            logs = jnp.sum(jnp.where(lane == 2 * c + h, log_total[...], 0.0), axis=1, keepdims=True)
            probs = jnp.exp(dot(query, key, 1, 1) * scale + bias[...] - logs)
            grad_probs = dot(grad_out, value, 1, 1)
            grad_scores = (probs * (grad_probs - jnp.sum(probs * grad_probs, axis=1, keepdims=True))).astype(LOW)
            grad_value = grad_value + dot(probs.astype(LOW), grad_out, 0, 0)
            grad_query.append(dot(grad_scores, key))
            grad_key = grad_key + dot(grad_scores, query, 0, 0)
        grad_q_pre[:, cols] = unrotate(jnp.where(left, grad_query[0], grad_query[1]) * scale).astype(LOW)
        grad_key = (grad_key + pltpu.roll(grad_key, HD, 1)) * scale
        return unrotate(grad_key), grad_value + pltpu.roll(grad_value, HD, 1)

    def two_groups(i):
        key_a, value_a = group(2 * i)
        key_b, value_b = group(2 * i + 1)
        at = pl.multiple_of(i * 128, 128)
        grad_kv_pre[:, pl.ds(at, 128)] = jnp.where(left, key_a, key_b).astype(LOW)
        at = pl.multiple_of(KV * HD + i * 128, 128)
        grad_kv_pre[:, pl.ds(at, 128)] = jnp.where(left, value_a, value_b).astype(LOW)

    def gather_rhs(i):
        rhs[:, pl.ds(0, 256)] = grad_q_pre[:, pl.ds(i * 256, 256)]
        rhs[:, pl.ds(256, 128)] = grad_kv_pre[:, pl.ds(i * 128, 128)]
        rhs[:, pl.ds(384, 128)] = grad_kv_pre[:, pl.ds(KV * HD + i * 128, 128)]

    for i in range(KV // 2):
        two_groups(i)
        gather_rhs(i)
        chunk_grads(2 + i, hidden, rhs)
        big.start(2 + i)
        if i == 0:
            big.paired(0)
            big.paired(1)
        if i == 1:
            big.paired(2)
        if i == 2:
            big.paired(3)
        if i == 3:
            big.met(0, 0)
            big.met(1, 0)
            big.paired(4)
            big.met(2, 0)

    for copy in loads[1:]:
        copy.wait()

    def hidden_tile(n, carry):
        cols = pl.ds(pl.multiple_of(n * tile, tile), tile)
        grad_hid[:, cols] = dot(grad_q_pre[...], query_full[cols, :], 1, 1) + dot(grad_kv_pre[...], keyval_full[cols, :], 1, 1)
        return carry

    lax.fori_loop(0, width // tile, hidden_tile, 0)
    big.paired(5)
    big.met(3, 0)
    big.met(0, 1)
    big.line(0)
    big.met(1, 1)
    big.line(1)
    back, gain1_sum = norm_back(x_ref[...].astype(F32), gain_row(0), grad_hid[...])
    input_grad[...] = input_grad[...] + back

    sub = lax.broadcasted_iota(jnp.int32, (16, width), 0)
    sums = jnp.where(sub == 0, gain1_sum, jnp.where(sub == 1, gain2_sum, 0.0))
    little_all = jnp.concatenate([grad_router, sums], axis=0).astype(LOW)
    for d in range(n_dp):
        for k in range(2):
            at = d * shard + k * side
            own_s[0, d, k] = little_all[:, at : at + side]
    little.start(0)
    big.met(2, 1)
    big.line(2)
    big.met(4, 0)
    little.paired(0)
    big.met(3, 1)
    big.line(3)
    big.met(5, 0)
    if with_late:
        for copy in late_loads:
            copy.wait()
        late.turn()
    little.met(0, 0)
    big.met(4, 1)
    big.line(4)
    little.met(0, 1)
    big.met(5, 1)
    big.line(5)
    def place(i, which, field):
        rows = pl.ds(pl.multiple_of(which * side, 16), side)
        if i < 2:
            add_rows(grad_o.at[rows, pl.ds(i * tile, tile)], field)
            return
        i = i - 2
        add_rows(grad_q.at[rows, pl.ds(i * 256, 256)], field.at[:, pl.ds(0, 256)])
        add_rows(grad_kv.at[rows, pl.ds(i * 128, 128)], field.at[:, pl.ds(256, 128)])
        add_rows(grad_kv.at[rows, pl.ds(KV * HD + i * 128, 128)], field.at[:, pl.ds(384, 128)])

    def settle(i):
        big.last(i).wait_recv()
        place(i, 1 - big.core, big.other.at[i])

    chunks = own.shape[0]
    hop = 2 * (big.depth - 1)
    for t in range(chunks, chunks + hop):
        big.line(t)
        little.line(t - chunks)
        if t >= hop:
            big.close(t - hop)
            place(t - hop, big.core, big.final.at[t - hop])
        if t > hop:
            settle(t - hop - 1)
        if with_late and t == chunks + hop // 2:
            late_end()
    little.line(hop)
    little.close(0)
    add_rows(grad_s.at[big.core], little.final.at[0])
    settle(chunks - 1)
    for i in range(chunks):
        big.finish(i)
    little.last(0).wait_recv()
    add_rows(grad_s.at[1 - big.core], little.other.at[0])
    little.finish(0)


def back(n_dp, n_exp, local, tokens, cotangent, hid_sum, gates_in, routes_t, parents, tables, saved, late, collective_id):
    tree, width = tokens.shape
    shard = width // n_dp
    shape, vm, sem = jax.ShapeDtypeStruct, pltpu.VMEM, pltpu.SemaphoreType.DMA
    side, chunks, tile, rows = shard // 2, 6, 512, EXPERTS + 16
    big_bufs, big_sems = GradSum.scratch(n_dp, chunks, side, tile)
    little_bufs, little_sems = GradSum.scratch(n_dp, 1, rows, side)
    args = (tokens, cotangent, hid_sum, gates_in, routes_t, parents, *tables, *saved)
    spaces = [VMEM] * len(args)
    spaces[16:19] = [ANY] * 3
    out_shape = [
        shape((tree, width), F32), shape((shard, width), F32), shape((shard, width), F32), shape((shard, width), F32),
        shape((2, rows, side), F32),
    ]
    extra = []
    if late is not None:
        args, spaces = (*args, late), spaces + [ANY]
        out_rows = late.shape[0] // n_dp - shard
        out_shape += [shape((shard, width), F32), shape((out_rows, width), F32)]
        extra = [sem((4,)), sem((6,)), sem((6,)), sem((2,)), vm((10 * late.shape[0] // (2 * n_dp), width), LOW)]
    return pl.pallas_call(
        functools.partial(back_body, n_dp, n_exp, local, late is not None),
        out_shape=out_shape,
        in_specs=[pl.BlockSpec(memory_space=s) for s in spaces],
        out_specs=[pl.BlockSpec(memory_space=s) for s in ([VMEM] * 5 + [ANY] * 2)[: len(out_shape)]],
        scratch_shapes=[
            vm((tree, tree), F32), vm((tree, width), LOW), vm((tree, width), LOW), vm((tree, width), LOW), vm((tree, width), LOW),
            vm((tree, tile), LOW), vm((chunks, n_dp, 2, side, tile), LOW), vm((1, n_dp, 2, rows, side), LOW),
            vm((tree, width), F32), vm((width, width), LOW), vm((width, width), LOW), vm((width, width), LOW), sem((3,)),
            *big_bufs, *big_sems, *little_bufs, *little_sems, *extra,
        ],
        compiler_params=pltpu.CompilerParams(
            collective_id=collective_id, has_side_effects=True, vmem_limit_bytes=63 * MIB),
        name="back",
    )(*args)


def rope_pairs(tree_rows):
    unit = tree_rows // 20
    row = np.arange(tree_rows)
    position = np.where(row < 8 * unit, row, np.where(row < 12 * unit, 8 * unit + row % unit, 9 * unit + row % unit))
    frequency = 10000.0 ** (-np.arange(0, HD, 2) / HD)
    angles = position[:, None] * frequency[None, :]
    return tuple(jnp.asarray(np.concatenate([table] * 4, axis=1), jnp.float32) for table in (np.cos(angles), np.sin(angles)))


def gated_unit(gate_up):
    width_ff = gate_up.shape[-1] // 2
    gate_part = gate_up[..., :width_ff]
    return gate_part / (1.0 + jnp.exp(-gate_part)) * gate_up[..., width_ff:]


def experts_plain(
    n_dp, n_exp, hidden2, grad_y, routes_all, router_full, expert_in, expert_out, middle
):
    tree_rows, width = hidden2.shape
    capacity = CAP
    routes_all = routes_all.transpose(0, 2, 1)
    expert_ids = jnp.arange(EXPERTS, dtype=jnp.int32)
    here = lax.axis_index("expert")
    local = expert_in.shape[0]
    first = here * local
    hidden_all = lax.all_gather(hidden2, "expert", axis=0, tiled=False)
    own_ids = first + jnp.arange(local, dtype=jnp.int32)
    hot_all = routes_all[:, :, :, None] == expert_ids[None, None, None, :]
    chosen_all = jnp.any(hot_all, axis=2)
    chosen = jnp.any(routes_all[:, :, :, None] == own_ids[None, None, None, :], axis=2)
    lower = jnp.tril(jnp.ones((tree_rows, tree_rows), jnp.bfloat16), -1)
    rank = jnp.einsum(
        "tu,jue->jet", lower, chosen.astype(jnp.bfloat16), preferred_element_type=jnp.float32
    ).astype(jnp.int32)
    slots = jnp.arange(capacity, dtype=jnp.int32)
    chosen_t = chosen.transpose(0, 2, 1)
    place = (rank[:, :, None, :] == slots[None, None, :, None]) & chosen_t[:, :, None, :]
    place = place.astype(jnp.bfloat16)
    logits_all = jnp.einsum(
        "jtd,de->jte", hidden_all, router_full, preferred_element_type=jnp.float32
    )
    masked = jnp.where(chosen_all, logits_all, -1e30)
    weight = jnp.exp(masked - jnp.max(masked, axis=-1, keepdims=True))
    weight = weight / jnp.sum(weight, axis=-1, keepdims=True)
    gates_own = lax.dynamic_slice_in_dim(weight, first, local, axis=2)
    gate_slot = jnp.einsum(
        "jest,jte->ejs", place.astype(jnp.float32), gates_own, precision=lax.Precision.HIGHEST
    )[..., None]
    sent = jnp.einsum("jest,jtd->ejsd", place, hidden_all, preferred_element_type=jnp.float32)
    sent = sent.astype(jnp.bfloat16)
    grad_rows = jnp.einsum("jest,jtd->ejsd", place, grad_y, preferred_element_type=jnp.float32)
    grad_rows = grad_rows.astype(jnp.bfloat16)
    gate_up = jnp.einsum("ejsd,edf->ejsf", sent, expert_in, preferred_element_type=jnp.float32)
    activated, glu_back = jax.vjp(gated_unit, gate_up)
    act_low = activated.astype(jnp.bfloat16).astype(jnp.float32)
    act_scaled = (act_low * gate_slot).astype(jnp.bfloat16)
    made = jnp.einsum(
        "ejsf,efd->ejsd", act_scaled, expert_out, preferred_element_type=jnp.float32
    ).astype(jnp.bfloat16)
    out_part = jnp.einsum("jest,ejsd->jtd", place, made, preferred_element_type=jnp.float32)
    out_sum = lax.psum_scatter(
        out_part.astype(jnp.bfloat16), "expert", scatter_dimension=0, tiled=False
    ).astype(jnp.float32)
    result = middle + out_sum
    block_out = result.astype(jnp.bfloat16)
    grad_act = jnp.einsum(
        "ejsd,efd->ejsf", grad_rows, expert_out, preferred_element_type=jnp.float32
    )
    gate_dot = jnp.sum(act_low * grad_act, axis=-1)
    gates_back = jnp.einsum(
        "jest,ejs->jte", place.astype(jnp.float32), gate_dot, precision=lax.Precision.HIGHEST
    )
    grad_out_w = jnp.einsum(
        "ejsf,ejsd->efd", act_scaled, grad_rows, preferred_element_type=jnp.float32
    )
    grad_gate_up = glu_back(grad_act * gate_slot)[0].astype(jnp.bfloat16)
    grad_sent = jnp.einsum(
        "ejsf,edf->ejsd", grad_gate_up, expert_in, preferred_element_type=jnp.float32
    ).astype(jnp.bfloat16)
    grad_in_w = jnp.einsum(
        "ejsd,ejsf->edf", sent, grad_gate_up, preferred_element_type=jnp.float32
    )
    hid_part = jnp.einsum("jest,ejsd->jtd", place, grad_sent, preferred_element_type=jnp.float32)
    gates_mine = lax.all_to_all(gates_back, "expert", split_axis=0, concat_axis=2, tiled=True)[0]
    hid_sum = lax.psum_scatter(
        hid_part.astype(jnp.bfloat16), "expert", scatter_dimension=0, tiled=False
    ).astype(jnp.float32)
    local, units = expert_in.shape[0], expert_out.shape[1]
    low = jnp.bfloat16
    grads = jnp.concatenate(
        [
            grad_in_w.astype(low).reshape(local, n_dp, width // n_dp, width),
            grad_out_w.astype(low).reshape(local, n_dp, units // n_dp, width),
        ],
        axis=2,
    ).reshape(local, width + units, width)
    share = lax.psum_scatter(grads, "dp", scatter_dimension=1, tiled=True).astype(jnp.float32)
    gates_mine = jnp.pad(gates_mine.T.reshape(n_exp, local, tree_rows), ((0, 0), (0, 8 - local), (0, 0)))
    return block_out, hid_sum, gates_mine, share[:, : width // n_dp], share[:, width // n_dp :]


def shards(
    tokens,
    attn_gain,
    w_query,
    w_keyval,
    w_output,
    moe_gain,
    w_router,
    expert_in,
    expert_out,
    cotangent,
    routes,
    parents,
):
    n_dp, n_exp = lax.axis_size("dp"), lax.axis_size("expert")
    local = expert_in.shape[0]
    tree_rows = tokens.shape[0]
    tables = rope_pairs(tree_rows)
    routes_t = routes.T
    (hidden, queries, keys, values, attended, middle, hidden2, log_total, *full, gains, routes_all, grad_y) = front(
        n_dp, n_exp, tokens, jnp.stack([attn_gain, moe_gain]), w_router.T, w_query, w_keyval, w_output, routes_t, parents, tables, cotangent, 1
    )
    router_t = full[3]
    if (n_dp, n_exp) == (4, 8):
        block_out, hid_sum, gate_grads, expert_in_share, expert_out_share, late = experts(
            n_dp, n_exp, hidden2, grad_y, routes_all, router_t, expert_in, expert_out, middle, 2
        )
    else:
        late = None
        block_out, hid_sum, gate_grads, expert_in_share, expert_out_share = experts_plain(
            n_dp, n_exp, hidden2, grad_y, routes_all, router_t[:EXPERTS].T, expert_in, expert_out, middle
        )
    saved = (hidden, queries, keys, values, attended, middle, hidden2, log_total, *full, gains)
    input_grad, grad_q, grad_kv, grad_o, grad_small, *made = back(
        n_dp, n_exp, local, tokens, cotangent, hid_sum, gate_grads.reshape(n_exp * 8, tree_rows), routes_t, parents, tables, saved, late, 3
    )
    if late is not None:
        expert_in_share = jnp.concatenate([expert_in_share, made[0][None]], axis=0)
        expert_out_share = jnp.concatenate([expert_out_share, made[1][None]], axis=0)
    return (
        block_out,
        input_grad,
        grad_small[:, EXPERTS].reshape(-1),
        grad_q,
        grad_kv,
        grad_o,
        grad_small[:, EXPERTS + 1].reshape(-1),
        jnp.concatenate([grad_small[0, :EXPERTS], grad_small[1, :EXPERTS]], axis=1).T,
        expert_in_share,
        expert_out_share,
    )


def solution(mesh):
    in_specs = (
        P(("dp", "expert"), None),
        P("dp"),
        P("dp", None),
        P("dp", None),
        P("dp", None),
        P("dp"),
        P("dp", None),
        P("expert", None, None),
        P("expert", None, None),
        P(("dp", "expert"), None),
        P(("dp", "expert"), None),
        P(("dp", "expert"), None),
    )
    out_specs = (
        P(("dp", "expert"), None),
        P(("dp", "expert"), None),
        P("dp"),
        P("dp", None),
        P("dp", None),
        P("dp", None),
        P("dp"),
        P("dp", None),
        P("expert", "dp", None),
        P("expert", "dp", None),
    )
    return jax.shard_map(shards, mesh=mesh, in_specs=in_specs, out_specs=out_specs, check_vma=False)
```

profile of v0, /device:TPU:0, one launch (start us, length us, event | category | flops | bytes accessed | tf_op | source)
XLA Modules:
  0.0 328.8 jit_solution(7260882910969598570)
XLA Ops:
  0.6 0.7 stack.9
  1.3 0.7 stack.10
  2.0 0.6 pad_maximum_fusion.2.gain_pair
  2.5 57.5 %front.1 = (bf16[320,1024]{1,0:T(8,128)(2,1)}, bf16[320,1024]{1,0:T(8,128)(2,1)}, bf16[8,320,128]{2,1,0:T(8,128)(2,1)}, bf16[8,320,128]{2,1,0:T(8,128)(2,1)}, bf...) custom-call(bf16[320,1024]{1,0:T(8,128)(2,1)} %x_ref.3, ...), custom_call_target="tpu_custom_call" | custom-call | tf_op jit(solution)/shard_map/front/pallas_call | solution.py:993
  60.0 174.3 %experts.1 = (bf16[320,1024]{1,0:T(8,128)(2,1)}, f32[320,1024]{1,0:T(8,128)}, f32[8,8,320]{2,1,0:T(8,128)}, f32[3,256,1024]{2,1,0:T(8,128)}, f32[3,128,1024]{2,1,0:T(8,128)}, /*index=5*/bf16[1536,1024]{1,0:T(8,128)(2,1)}) custom-call(bf16[320,1024]{1,0:T(8,128)(2,1)} %get-tuple-element.38.hid_ref.hidden2, bf16[8,320,1024]{2,1,0:T(8,128)(2,1)} %get-tuple-element.39.gy_hbm, ...), custom_call_target="tpu_custom_call" | custom-call | tf_op jit(solution)/shard_map/experts/pallas_call | solution.py:683
  234.3 80.2 %back.1 = (f32[320,1024]{1,0:T(8,128)}, f32[256,1024]{1,0:T(8,128)}, f32[256,1024]{1,0:T(8,128)}, f32[256,1024]{1,0:T(8,128)}, f32[2,48,128]{2,1,0:T(8,128)}, /*index=5*/f32[256,1024]{1,0:T(8,128)}, f32[128,1024]{1,0:T(8,128)}) custom-call(bf16[320,1024]{1,0:T(8,128)(2,1)} %x_ref.3, bf16[320,1024]{1,0:T(8,128)(2,1)} %cot.3, ...), custom_call_target="tpu_custom_call" | custom-call | tf_op jit(solution)/shard_map/back/pallas_call | solution.py:1444
  314.5 1.3 fusion
  315.8 0.7 slice_bitcast_fusion.1
  316.6 0.6 maximum_bitcast_fusion
  317.2 0.0 copy-start
  317.2 0.0 copy-start.5
  317.2 3.3 pad_maximum_fusion.1
  320.5 0.0 copy-done
  320.5 0.0 copy-done.5
  320.5 0.0 copy-start.6
  320.5 2.3 pad_maximum_fusion
  322.8 0.0 copy-done.6
  322.8 0.0 copy-start.1
  322.8 0.0 copy-start.4
  322.8 0.8 copy.29
  323.7 0.7 copy-done.1
  324.4 0.0 copy-start.3
  324.4 1.1 copy.30
  325.4 0.0 copy-done.4
  325.4 0.0 copy-start.2
  325.4 1.0 copy.31
  326.4 0.0 copy-done.3
  326.4 1.0 copy.32
  327.4 0.0 copy-done.2
  327.4 1.0 copy.33
Async XLA Ops:
  317.2 3.3 %copy-start = (f32[3,256,1024]{2,1,0:T(8,128)S(1)}, f32[3,256,1024]{2,1,0:T(8,128)}, u32[]{:S(2)}) copy-start(f32[3,256,1024]{2,1,0:T(8,128)} %get-tuple-element.62) | copy-start | bytes 9437188
  317.2 3.3 %copy-start.5 = (f32[256,1024]{1,0:T(8,128)S(1)}, f32[256,1024]{1,0:T(8,128)}, u32[]{:S(2)}) copy-start(f32[256,1024]{1,0:T(8,128)} %get-tuple-element.63) | copy-start | bytes 3145732
  320.5 2.3 copy-start.6
  322.8 1.6 copy-start.1
  322.8 2.6 copy-start.4
  324.4 2.0 copy-start.3
  325.4 1.9 copy-start.2
where the time goes:
time: 335 us; the launch traced here: 329 us
  Pallas kernels  312 us (93%)
  local copies, waits for them, and re-layouts  8.94 us (3%)
  other arithmetic  6.79 us (2%)
    pallas_call x1, Pallas kernels, experts(): pl.pallas_call(functools.partial(experts_body, n_dp, n_exp), out_shape=[s...  174 us
    pallas_call x1, Pallas kernels, back(): pl.pallas_call(functools.partial(back_body, n_dp, n_exp, local, late is n...  80.2 us
    pallas_call x1, Pallas kernels, front(): pl.pallas_call(functools.partial(front_body, n_dp, n_exp), out_shape=[low...  57.5 us

commit v1 on v0

--- a/solution.py
+++ b/solution.py
@@ -473,6 +473,7 @@
         def _():
             for event in events[4:]:
                 gather.handle(event)
+            out.early()
             gather.wait_pair(2, 0)
             gather.wait_pair(2, 1)
 
@@ -499,7 +500,6 @@
 
     lax.fori_loop(0, depth, group, 0)
     out.first()
-    out.early()
     middle_copy = pltpu.make_async_copy(middle, wide.at[pl.ds(0, tree)], wide_sem.at[0])
     middle_copy.start()
 
@@ -889,10 +889,10 @@
         gather.turn(0, j)
         gather.turn(1, j)
     gather.start(2)
+    for event in events[:2]:
+        ring.handle(event)
     gather.turn(0, stages - 1)
     gather.turn(1, stages - 1)
-    for event in events[:2]:
-        ring.handle(event)
     gather.ready(0)
     saves[0].start()
 

time: 335 us -> 331 us (0.988)
  Pallas kernels: 312 us -> 308 us
where the time goes in v1:
time: 331 us; the launch traced here: 325 us
  Pallas kernels  308 us (93%)
  local copies, waits for them, and re-layouts  8.94 us (3%)
  other arithmetic  6.79 us (2%)
    pallas_call x1, Pallas kernels, experts(): pl.pallas_call(functools.partial(experts_body, n_dp, n_exp), out_shape=[s...  173 us
    pallas_call x1, Pallas kernels, back(): pl.pallas_call(functools.partial(back_body, n_dp, n_exp, local, late is n...  78.3 us
    pallas_call x1, Pallas kernels, front(): pl.pallas_call(functools.partial(front_body, n_dp, n_exp), out_shape=[low...  57.5 us

profile of v1, /device:TPU:0, one launch (start us, length us, event | category | flops | bytes accessed | tf_op | source)
XLA Modules:
  0.0 325.3 jit_solution(10253769746362561722)
XLA Ops:
  0.6 0.7 stack.9
  1.3 0.7 stack.10
  2.0 0.6 pad_maximum_fusion.2.gain_pair
  2.5 57.5 %front.1 = (bf16[320,1024]{1,0:T(8,128)(2,1)}, bf16[320,1024]{1,0:T(8,128)(2,1)}, bf16[8,320,128]{2,1,0:T(8,128)(2,1)}, bf16[8,320,128]{2,1,0:T(8,128)(2,1)}, bf...) custom-call(bf16[320,1024]{1,0:T(8,128)(2,1)} %x_ref.3, ...), custom_call_target="tpu_custom_call" | custom-call | tf_op jit(solution)/shard_map/front/pallas_call | solution.py:993
  60.0 172.7 %experts.1 = (bf16[320,1024]{1,0:T(8,128)(2,1)}, f32[320,1024]{1,0:T(8,128)}, f32[8,8,320]{2,1,0:T(8,128)}, f32[3,256,1024]{2,1,0:T(8,128)}, f32[3,128,1024]{2,1,0:T(8,128)}, /*index=5*/bf16[1536,1024]{1,0:T(8,128)(2,1)}) custom-call(bf16[320,1024]{1,0:T(8,128)(2,1)} %get-tuple-element.38.hid_ref.hidden2, bf16[8,320,1024]{2,1,0:T(8,128)(2,1)} %get-tuple-element.39.gy_hbm, ...), custom_call_target="tpu_custom_call" | custom-call | tf_op jit(solution)/shard_map/experts/pallas_call | solution.py:683
  232.7 78.3 %back.1 = (f32[320,1024]{1,0:T(8,128)}, f32[256,1024]{1,0:T(8,128)}, f32[256,1024]{1,0:T(8,128)}, f32[256,1024]{1,0:T(8,128)}, f32[2,48,128]{2,1,0:T(8,128)}, /*index=5*/f32[256,1024]{1,0:T(8,128)}, f32[128,1024]{1,0:T(8,128)}) custom-call(bf16[320,1024]{1,0:T(8,128)(2,1)} %x_ref.3, bf16[320,1024]{1,0:T(8,128)(2,1)} %cot.3, ...), custom_call_target="tpu_custom_call" | custom-call | tf_op jit(solution)/shard_map/back/pallas_call | solution.py:1444
  311.0 1.3 fusion
  312.3 0.7 slice_bitcast_fusion.1
  313.1 0.6 maximum_bitcast_fusion
  313.7 0.0 copy-start
  313.7 0.0 copy-start.5
  313.7 3.3 %pad_maximum_fusion.1 = f32[4,128,1024]{2,1,0:T(8,128)} fusion(f32[1,128,1024]{2,1,0:T(8,128)} %bitcast.14, f32[3,128,1024]{2,1,0:T(8,128)} %get-tuple-element.64), kind=kLoop, calls=%fused_computation.1 | loop fusion | flops 524288 | bytes 4194304 | tf_op jit(solution)/shard_map/concatenate | solution.py:1600
  317.0 0.0 copy-done
  317.0 0.0 copy-done.5
  317.0 0.0 copy-start.6
  317.0 2.3 pad_maximum_fusion
  319.3 0.0 copy-done.6
  319.3 0.0 copy-start.1
  319.3 0.0 copy-start.4
  319.3 0.8 copy.29
  320.1 0.7 copy-done.1
  320.9 0.0 copy-start.3
  320.9 1.1 copy.30
  321.9 0.0 copy-done.4
  321.9 0.0 copy-start.2
  321.9 1.0 copy.31
  322.9 0.0 copy-done.3
  322.9 1.0 copy.32
  323.9 0.0 copy-done.2
  323.9 1.0 copy.33
Async XLA Ops:
  313.7 3.3 %copy-start = (f32[3,256,1024]{2,1,0:T(8,128)S(1)}, f32[3,256,1024]{2,1,0:T(8,128)}, u32[]{:S(2)}) copy-start(f32[3,256,1024]{2,1,0:T(8,128)} %get-tuple-element.62) | copy-start | bytes 9437188
  313.7 3.3 %copy-start.5 = (f32[256,1024]{1,0:T(8,128)S(1)}, f32[256,1024]{1,0:T(8,128)}, u32[]{:S(2)}) copy-start(f32[256,1024]{1,0:T(8,128)} %get-tuple-element.63) | copy-start | bytes 3145732
  317.0 2.3 copy-start.6
  319.3 1.6 copy-start.1
  319.3 2.6 copy-start.4
  320.9 2.0 copy-start.3
  321.9 1.9 copy-start.2

commit v2 on v1

--- a/solution.py
+++ b/solution.py
@@ -45,8 +45,9 @@
     pl.semaphore_wait(barrier, count)
 
 
-def add_rows(out, *terms, step=16):
+def add_rows(out, *terms):
     rows = out.shape[0]
+    step = 32 if rows % 32 == 0 else 16
 
     def body(i, carry):
         at = pl.ds(pl.multiple_of(i * step, step), step)
@@ -420,14 +421,9 @@
 
         lax.fori_loop(0, local, one_expert, 0)
 
-    def combine_out(chip):
-        def one_tree(q, carry):
-            j = 2 * chip + q
-            rows = pl.ds(pl.multiple_of(q * rows_e, rows_e), rows_e)
-            x_all[j] = dot(places_t(j), tmp[rows, :]).astype(LOW)
-            return carry
-
-        lax.fori_loop(0, 2, one_tree, 0)
+    def combine_out(chip, q):
+        rows = pl.ds(pl.multiple_of(q * rows_e, rows_e), rows_e)
+        x_all[2 * chip + q] = dot(places_t(2 * chip + q), tmp[rows, :]).astype(LOW)
 
     def grad_rows(j, carry):
         pl.when(j + 1 < n_exp)(lambda: gy_copy(j + 1).start())
@@ -491,11 +487,12 @@
                     if event[1] == abs(d) and (abs(d) == 2 or (event[0] == 0) == (d < 0)):
                         gather.finish_event(event)
 
-        combine_out(chip)
+        combine_out(chip, 1 - core)
         pl.when(g == 0)(lambda: out.start_pair(0))
         pl.when(g == 1)(lambda: out.start_pair(depth - 1))
         pl.when(g == 2)(lambda: out.start_pair(1))
         pl.when(g == 3)(lambda: out.start_pair(2))
+        combine_out(chip, core)
         return carry
 
     lax.fori_loop(0, depth, group, 0)
@@ -595,7 +592,6 @@
         for bit in (1, 2):
             pl.semaphore_signal(dp_ready.at[e], inc=1, device_id={"dp": me ^ bit}, device_id_type=MESH)
         pl.when(e == 1)(out.late)
-        pl.when(e >= 2)(lambda: grads_turn(e - 2))
         return carry
 
     dots[...] = jnp.zeros(dots.shape, F32)
@@ -651,6 +647,7 @@
         for h in range(2):
             late_copy(r, h).start()
     hid.late()
+    grads_turn(0)
     grads_turn(end - 2)
     grads_end(0)
     grads_turn(end - 1)
@@ -829,9 +826,10 @@
 
 
 def front_body(n_dp, n_exp, x_ref, gain_pair, router_in, w_query, w_keyval, w_output, routes_t, parents, cosine, sine, cot,
-               hidden_hbm, queries_hbm, keys_hbm, values_hbm, attended, middle, hidden2, log_total,
+               hidden_hbm, queries_hbm, keys_hbm, values_hbm, attended_hbm, middle_hbm, hidden2_hbm, log_hbm,
                query_hbm, keyval_hbm, output_hbm, router_t, gains, routes_all, grad_y,
-               hidden, queries, keys, values, query_full, keyval_full, output_full, small, small_all, bias, *sems):
+               hidden, queries, keys, values, query_full, keyval_full, output_full, small, small_all, bias,
+               attended, middle, hidden2, log_total, *sems):
     gather_sems, (small_send, small_recv, route_send, route_recv, out_sem), ring_sems = sems[:5], sems[5:10], sems[10:14]
     me, mine = lax.axis_index("dp"), lax.axis_index("expert")
     peers = [lax.rem(mine + k, n_exp) for k in range(1, n_exp)]
@@ -857,7 +855,8 @@
         pltpu.make_async_copy(src, dst, out_sem.at[k])
         for k, (src, dst) in enumerate((
             (query_full, query_hbm), (keyval_full, keyval_hbm), (output_full, output_hbm), (hidden, hidden_hbm),
-            (queries, queries_hbm), (keys, keys_hbm), (values, values_hbm), (cot, grad_y.at[mine])))
+            (queries, queries_hbm), (keys, keys_hbm), (values, values_hbm), (cot, grad_y.at[mine]),
+            (attended, attended_hbm), (log_total, log_hbm), (middle, middle_hbm), (hidden2, hidden2_hbm)))
     ]
     ring = RingGather(Ring(n_exp), cot, grad_y, ring_sems)
     events = ring.events()
@@ -949,6 +948,8 @@
         return carry
 
     lax.fori_loop(0, KV, heads, 0)
+    saves[8].start()
+    saves[9].start()
     for event in events[2:4]:
         ring.handle(event)
     gather.ready(2)
@@ -960,8 +961,10 @@
         return carry
 
     lax.fori_loop(0, width // tile, middle_tile, 0)
+    saves[10].start()
     field = middle[...]
     hidden2[...] = (field * inverse_rms(field) * gain_rows[1:2]).astype(LOW)
+    saves[11].start()
     for a in range(3):
         gather.finish(a)
     for k in range(1, n_dp):
@@ -998,12 +1001,13 @@
             shape((n_exp,) + routes_t.shape, jnp.int32), shape((n_exp, tree, width), LOW),
         ],
         in_specs=[pl.BlockSpec(memory_space=VMEM)] * 11,
-        out_specs=[pl.BlockSpec(memory_space=s) for s in [ANY] * 4 + [VMEM] * 4 + [ANY] * 3 + [VMEM] * 3 + [ANY]],
+        out_specs=[pl.BlockSpec(memory_space=s) for s in [ANY] * 11 + [VMEM] * 3 + [ANY]],
         scratch_shapes=[
             vm((tree, width), LOW), vm((tree, width), LOW), vm(spread.shape, LOW), vm(spread.shape, LOW),
             vm(full.shape, LOW), vm(full.shape, LOW), vm(full.shape, LOW),
             vm(small, LOW), vm((n_dp,) + small, LOW), vm((tree, tree), F32),
-            *DpGather.scratch(3, n_dp), sem((n_dp,)), sem((n_dp,)), sem((n_exp - 1,)), sem((n_exp - 1,)), sem((8,)),
+            vm((tree, width), LOW), vm((tree, width), F32), vm((tree, width), LOW), vm((tree, 128), F32),
+            *DpGather.scratch(3, n_dp), sem((n_dp,)), sem((n_dp,)), sem((n_exp - 1,)), sem((n_exp - 1,)), sem((12,)),
             *RingGather.scratch(n_exp),
         ],
         compiler_params=pltpu.CompilerParams(
@@ -1175,9 +1179,9 @@
     if with_late:
         late_hbm, refs = refs[0], refs[1:]
     outs, refs = refs[: 5 + 2 * with_late], refs[5 + 2 * with_late :]
-    input_grad, grad_q, grad_kv, grad_o, grad_s = outs[:5]
+    input_hbm, grad_q, grad_kv, grad_o, grad_s = outs[:5]
     (bias, branch, grad_att, grad_q_pre, grad_kv_pre, rhs, own, own_s, grad_hid, query_full, keyval_full, output_full,
-     load_sem, *rest) = refs
+     load_sem, input_grad, *rest) = refs
     big = GradSum(n_dp, n_exp, own.shape[0], own, rest[:8], rest[8:18])
     little = GradSum(n_dp, n_exp, 1, own_s, rest[18:26], rest[26:36])
     tree, width = x_ref.shape
@@ -1358,6 +1362,8 @@
     big.line(1)
     back, gain1_sum = norm_back(x_ref[...].astype(F32), gain_row(0), grad_hid[...])
     input_grad[...] = input_grad[...] + back
+    input_copy = pltpu.make_async_copy(input_grad, input_hbm, load_sem.at[3])
+    input_copy.start()
 
     sub = lax.broadcasted_iota(jnp.int32, (16, width), 0)
     sums = jnp.where(sub == 0, gain1_sum, jnp.where(sub == 1, gain2_sum, 0.0))
@@ -1419,6 +1425,7 @@
     little.last(0).wait_recv()
     add_rows(grad_s.at[1 - big.core], little.other.at[0])
     little.finish(0)
+    input_copy.wait()
 
 
 def back(n_dp, n_exp, local, tokens, cotangent, hid_sum, gates_in, routes_t, parents, tables, saved, late, collective_id):
@@ -1445,11 +1452,11 @@
         functools.partial(back_body, n_dp, n_exp, local, late is not None),
         out_shape=out_shape,
         in_specs=[pl.BlockSpec(memory_space=s) for s in spaces],
-        out_specs=[pl.BlockSpec(memory_space=s) for s in ([VMEM] * 5 + [ANY] * 2)[: len(out_shape)]],
+        out_specs=[pl.BlockSpec(memory_space=s) for s in ([ANY] + [VMEM] * 4 + [ANY] * 2)[: len(out_shape)]],
         scratch_shapes=[
             vm((tree, tree), F32), vm((tree, width), LOW), vm((tree, width), LOW), vm((tree, width), LOW), vm((tree, width), LOW),
             vm((tree, tile), LOW), vm((chunks, n_dp, 2, side, tile), LOW), vm((1, n_dp, 2, rows, side), LOW),
-            vm((tree, width), F32), vm((width, width), LOW), vm((width, width), LOW), vm((width, width), LOW), sem((3,)),
+            vm((tree, width), F32), vm((width, width), LOW), vm((width, width), LOW), vm((width, width), LOW), sem((4,)), vm((tree, width), F32),
             *big_bufs, *big_sems, *little_bufs, *little_sems, *extra,
         ],
         compiler_params=pltpu.CompilerParams(

time: 331 us -> 327 us (0.988)
  Pallas kernels: 308 us -> 304 us
where the time goes in v2:
time: 327 us; the launch traced here: 320 us
  Pallas kernels  304 us (93%)
  local copies, waits for them, and re-layouts  8.94 us (3%)
  other arithmetic  6.79 us (2%)
    pallas_call x1, Pallas kernels, experts(): pl.pallas_call(functools.partial(experts_body, n_dp, n_exp), out_shape=[s...  170 us
    pallas_call x1, Pallas kernels, back(): pl.pallas_call(functools.partial(back_body, n_dp, n_exp, local, late is n...  77.6 us
    pallas_call x1, Pallas kernels, front(): pl.pallas_call(functools.partial(front_body, n_dp, n_exp), out_shape=[low...  56.5 us

profile of v2, /device:TPU:0, one launch (start us, length us, event | category | flops | bytes accessed | tf_op | source)
XLA Modules:
  0.0 320.2 jit_solution(1238379863167932801)
XLA Ops:
  0.6 0.7 stack.9
  1.3 0.7 stack.10
  2.0 0.6 pad_maximum_fusion.2.gain_pair
  2.5 56.5 %front.1 = (bf16[320,1024]{1,0:T(8,128)(2,1)}, bf16[320,1024]{1,0:T(8,128)(2,1)}, bf16[8,320,128]{2,1,0:T(8,128)(2,1)}, bf16[8,320,128]{2,1,0:T(8,128)(2,1)}, bf...) custom-call(bf16[320,1024]{1,0:T(8,128)(2,1)} %x_ref.3, ...), custom_call_target="tpu_custom_call" | custom-call | tf_op jit(solution)/shard_map/front/pallas_call | solution.py:996
  59.0 169.5 %experts.1 = (bf16[320,1024]{1,0:T(8,128)(2,1)}, f32[320,1024]{1,0:T(8,128)}, f32[8,8,320]{2,1,0:T(8,128)}, f32[3,256,1024]{2,1,0:T(8,128)}, f32[3,128,1024]{2,1,0:T(8,128)}, /*index=5*/bf16[1536,1024]{1,0:T(8,128)(2,1)}) custom-call(bf16[320,1024]{1,0:T(8,128)(2,1)} %get-tuple-element.38.hid_ref.hidden2, bf16[8,320,1024]{2,1,0:T(8,128)(2,1)} %get-tuple-element.39.gy_hbm, ...), custom_call_target="tpu_custom_call" | custom-call | tf_op jit(solution)/shard_map/experts/pallas_call | solution.py:680
  228.6 77.6 %back.1 = (f32[320,1024]{1,0:T(8,128)}, f32[256,1024]{1,0:T(8,128)}, f32[256,1024]{1,0:T(8,128)}, f32[256,1024]{1,0:T(8,128)}, f32[2,48,128]{2,1,0:T(8,128)}, /*index=5*/f32[256,1024]{1,0:T(8,128)}, f32[128,1024]{1,0:T(8,128)}) custom-call(bf16[320,1024]{1,0:T(8,128)(2,1)} %x_ref.3, bf16[320,1024]{1,0:T(8,128)(2,1)} %cot.3, ...), custom_call_target="tpu_custom_call" | custom-call | tf_op jit(solution)/shard_map/back/pallas_call | solution.py:1451
  306.1 1.3 fusion
  307.5 0.7 slice_bitcast_fusion.1
  308.2 0.6 maximum_bitcast_fusion
  308.8 0.0 copy-start
  308.8 0.0 copy-start.5
  308.8 3.3 %pad_maximum_fusion.1 = f32[4,128,1024]{2,1,0:T(8,128)} fusion(f32[1,128,1024]{2,1,0:T(8,128)} %bitcast.14, f32[3,128,1024]{2,1,0:T(8,128)} %get-tuple-element.64), kind=kLoop, calls=%fused_computation.1 | loop fusion | flops 524288 | bytes 4194304 | tf_op jit(solution)/shard_map/concatenate | solution.py:1607
  312.1 0.0 copy-done
  312.1 0.0 copy-done.5
  312.1 0.0 copy-start.6
  312.1 2.3 pad_maximum_fusion
  314.5 0.0 copy-done.6
  314.5 0.0 copy-start.1
  314.5 0.0 copy-start.4
  314.5 0.8 copy.29
  315.3 0.7 copy-done.1
  316.0 0.0 copy-start.3
  316.0 1.1 copy.30
  317.1 0.0 copy-done.4
  317.1 0.0 copy-start.2
  317.1 1.0 copy.31
  318.0 0.0 copy-done.3
  318.0 1.0 copy.32
  319.0 0.0 copy-done.2
  319.0 1.0 copy.33
Async XLA Ops:
  308.8 3.3 %copy-start = (f32[3,256,1024]{2,1,0:T(8,128)S(1)}, f32[3,256,1024]{2,1,0:T(8,128)}, u32[]{:S(2)}) copy-start(f32[3,256,1024]{2,1,0:T(8,128)} %get-tuple-element.62) | copy-start | bytes 9437188
  308.8 3.3 %copy-start.5 = (f32[256,1024]{1,0:T(8,128)S(1)}, f32[256,1024]{1,0:T(8,128)}, u32[]{:S(2)}) copy-start(f32[256,1024]{1,0:T(8,128)} %get-tuple-element.63) | copy-start | bytes 3145732
  312.1 2.3 copy-start.6
  314.5 1.6 copy-start.1
  314.5 2.6 copy-start.4
  316.0 2.0 copy-start.3
  317.1 1.9 copy-start.2

commit v3 on v2

--- a/solution.py
+++ b/solution.py
@@ -616,8 +616,6 @@
             made = jnp.concatenate([sent[i, rows, :] for i in range(end)] + [grows[end - 1, rows, :]], axis=0)
             hid_part(d, other)[...] = dot(places_t(j), made).astype(LOW)
 
-    for d in (2, 1, depth - 1):
-        combine_hid(d)
 
     gate_copies = []
     for k, e in enumerate(peers):
@@ -630,10 +628,14 @@
     out.finish_sends()
     for partner in (ring.pair, ring.right, ring.left):
         pl.semaphore_signal(ready, inc=1, device_id={"expert": partner}, device_id_type=MESH)
+    combine_hid(2)
     pl.semaphore_wait(ready, 3)
-    for d in (2, 1, depth - 1):
-        hid.start_pair(d)
+    hid.start_pair(2)
+    combine_hid(1)
+    hid.start_pair(1)
     hid.first()
+    combine_hid(depth - 1)
+    hid.start_pair(depth - 1)
     combine_hid(0)
     hid.start_pair(0)
     hid.early()

time: 327 us -> 327 us (level)
  no operation moved by 1% of the time
where the time goes in v3:
time: 327 us; the launch traced here: 321 us
  Pallas kernels  304 us (93%)
  local copies, waits for them, and re-layouts  8.94 us (3%)
  other arithmetic  6.79 us (2%)
    pallas_call x1, Pallas kernels, experts(): pl.pallas_call(functools.partial(experts_body, n_dp, n_exp), out_shape=[s...  169 us
    pallas_call x1, Pallas kernels, back(): pl.pallas_call(functools.partial(back_body, n_dp, n_exp, local, late is n...  77.6 us
    pallas_call x1, Pallas kernels, front(): pl.pallas_call(functools.partial(front_body, n_dp, n_exp), out_shape=[low...  56.5 us

profile of v3, /device:TPU:0, one launch (start us, length us, event | category | flops | bytes accessed | tf_op | source)
XLA Modules:
  0.0 320.5 jit_solution(8050773446685644829)
XLA Ops:
  0.6 0.7 stack.9
  1.3 0.7 stack.10
  2.0 0.6 pad_maximum_fusion.2.gain_pair
  2.5 56.5 %front.1 = (bf16[320,1024]{1,0:T(8,128)(2,1)}, bf16[320,1024]{1,0:T(8,128)(2,1)}, bf16[8,320,128]{2,1,0:T(8,128)(2,1)}, bf16[8,320,128]{2,1,0:T(8,128)(2,1)}, bf...) custom-call(bf16[320,1024]{1,0:T(8,128)(2,1)} %x_ref.3, ...), custom_call_target="tpu_custom_call" | custom-call | tf_op jit(solution)/shard_map/front/pallas_call | solution.py:998
  59.0 169.5 %experts.1 = (bf16[320,1024]{1,0:T(8,128)(2,1)}, f32[320,1024]{1,0:T(8,128)}, f32[8,8,320]{2,1,0:T(8,128)}, f32[3,256,1024]{2,1,0:T(8,128)}, f32[3,128,1024]{2,1,0:T(8,128)}, /*index=5*/bf16[1536,1024]{1,0:T(8,128)(2,1)}) custom-call(bf16[320,1024]{1,0:T(8,128)(2,1)} %get-tuple-element.38.hid_ref.hidden2, bf16[8,320,1024]{2,1,0:T(8,128)(2,1)} %get-tuple-element.39.gy_hbm, ...), custom_call_target="tpu_custom_call" | custom-call | tf_op jit(solution)/shard_map/experts/pallas_call | solution.py:682
  228.5 77.6 %back.1 = (f32[320,1024]{1,0:T(8,128)}, f32[256,1024]{1,0:T(8,128)}, f32[256,1024]{1,0:T(8,128)}, f32[256,1024]{1,0:T(8,128)}, f32[2,48,128]{2,1,0:T(8,128)}, /*index=5*/f32[256,1024]{1,0:T(8,128)}, f32[128,1024]{1,0:T(8,128)}) custom-call(bf16[320,1024]{1,0:T(8,128)(2,1)} %x_ref.3, bf16[320,1024]{1,0:T(8,128)(2,1)} %cot.3, ...), custom_call_target="tpu_custom_call" | custom-call | tf_op jit(solution)/shard_map/back/pallas_call | solution.py:1453
  306.2 1.3 fusion
  307.5 0.7 slice_bitcast_fusion.1
  308.3 0.6 maximum_bitcast_fusion
  308.9 0.0 copy-start
  308.9 0.0 copy-start.5
  308.9 3.3 %pad_maximum_fusion.1 = f32[4,128,1024]{2,1,0:T(8,128)} fusion(f32[1,128,1024]{2,1,0:T(8,128)} %bitcast.14, f32[3,128,1024]{2,1,0:T(8,128)} %get-tuple-element.64), kind=kLoop, calls=%fused_computation.1 | loop fusion | flops 524288 | bytes 4194304 | tf_op jit(solution)/shard_map/concatenate | solution.py:1609
  312.2 0.0 copy-done
  312.2 0.0 copy-done.5
  312.2 0.0 copy-start.6
  312.2 2.3 pad_maximum_fusion
  314.5 0.0 copy-done.6
  314.5 0.0 copy-start.1
  314.5 0.0 copy-start.4
  314.5 0.8 copy.29
  315.3 0.7 copy-done.1
  316.1 0.0 copy-start.3
  316.1 1.1 copy.30
  317.1 0.0 copy-done.4
  317.1 0.0 copy-start.2
  317.1 1.0 copy.31
  318.1 0.0 copy-done.3
  318.1 1.0 copy.32
  319.1 0.0 copy-done.2
  319.1 1.0 copy.33
Async XLA Ops:
  308.9 3.3 %copy-start = (f32[3,256,1024]{2,1,0:T(8,128)S(1)}, f32[3,256,1024]{2,1,0:T(8,128)}, u32[]{:S(2)}) copy-start(f32[3,256,1024]{2,1,0:T(8,128)} %get-tuple-element.62) | copy-start | bytes 9437188
  308.9 3.3 %copy-start.5 = (f32[256,1024]{1,0:T(8,128)S(1)}, f32[256,1024]{1,0:T(8,128)}, u32[]{:S(2)}) copy-start(f32[256,1024]{1,0:T(8,128)} %get-tuple-element.63) | copy-start | bytes 3145732
  312.2 2.3 copy-start.6
  314.5 1.6 copy-start.1
  314.5 2.6 copy-start.4
  316.1 2.0 copy-start.3
  317.1 1.9 copy-start.2
